TPU v7x, 32 devices: a whole 2x2x4 slice. The times are simulated.
32 devices in a mesh: rep: 4 (over x, core), shard: 8 (over z, y).
Axes of the slice: x: 2, y: 2, z: 4, core: 2. Of those that a mesh axis runs over, the one named last changes fastest.
Arguments:
- layer_input: bfloat16 [4096, 8192], P(('rep', 'shard')), may hold values from -6 to 6
- queries: bfloat16 [4096, 512], P(('rep', 'shard')), may hold values from -10 to 10
- d_out: bfloat16 [4096, 512], P(('rep', 'shard')), may hold values from -6 to 6
- segment_ids: int32 [32, 128], P(('rep', 'shard')), may hold values from 0 to 3, never falling along the last dimension, each value on 1 to 64 neighbouring positions
- kv_weight: bfloat16 [8192, 256], P('shard'), may hold values from -0.0625 to 0.0625
Outputs:
- d_input: bfloat16 [4096, 8192], P(('rep', 'shard'))
- d_queries: bfloat16 [4096, 512], P(('rep', 'shard'))
- d_kv_weight: float32 [8192, 256], P('shard')
All inputs are finite; a program needn't handle non-finite values.
Results may differ from a plain program's by a relative error of at most 0.03.
Values may be sent and summed in bfloat16 or wider, within the bound.
No kernel may reach another device: no remote copies, remote signals or barrier semaphores. Data moves between devices by JAX's collectives and lax.ppermute only.
A program may use at most 64 MiB of HBM per device.

v0:
```python
import jax
import jax.numpy as jnp
from jax import lax
from jax.sharding import PartitionSpec as P

HEAD = 128
QH = 4


def attention_grad(queries, keyval, d_out, segment):
    rows = queries.shape[0]
    scale = 1.0 / HEAD**0.5
    heads = queries.reshape(rows, QH, HEAD)
    grads = d_out.reshape(rows, QH, HEAD)
    keys = keyval[:, :HEAD]
    values = keyval[:, HEAD:]
    position = jnp.arange(rows)
    allowed = (segment[:, None] == segment[None, :]) & (position[None, :] <= position[:, None])
    scores = jnp.einsum("thd,sd->hts", heads, keys, preferred_element_type=jnp.float32) * scale
    scores = jnp.where(allowed[None], scores, -1e30)
    top = jnp.max(scores, axis=2, keepdims=True)
    weights = jnp.where(allowed[None], jnp.exp(scores - top), 0.0)
    probs = weights / jnp.sum(weights, axis=2, keepdims=True)
    probs_low = probs.astype(jnp.bfloat16)
    attended = jnp.einsum("hts,sd->thd", probs_low, values, preferred_element_type=jnp.float32)
    delta = jnp.sum(grads.astype(jnp.float32) * attended, axis=2)
    dprob = jnp.einsum("thd,sd->hts", grads, values, preferred_element_type=jnp.float32)
    dscore = (probs * (dprob - jnp.transpose(delta)[:, :, None])).astype(jnp.bfloat16)
    d_queries = (
        jnp.einsum("hts,sd->thd", dscore, keys, preferred_element_type=jnp.float32) * scale
    ).astype(jnp.bfloat16)
    d_keys = jnp.einsum("hts,thd->sd", dscore, heads, preferred_element_type=jnp.float32) * scale
    d_values = jnp.einsum("hts,thd->sd", probs_low, grads, preferred_element_type=jnp.float32)
    d_keyval = jnp.concatenate([d_keys, d_values], axis=1).astype(jnp.bfloat16)
    return (d_queries.reshape(rows, QH * HEAD), d_keyval)


def transposed_product(left, right):
    return lax.dot_general(
        left, right, (((1,), (1,)), ((), ())), preferred_element_type=jnp.float32
    )


def body(layer_input, queries, d_out, segment_ids, kv_weight):
    columns = layer_input
    keyval = jnp.dot(
        columns,
        lax.all_gather(kv_weight, "shard", axis=0, tiled=True),
        preferred_element_type=jnp.float32,
    ).astype(jnp.bfloat16)
    d_queries, d_keyval = attention_grad(queries, keyval, d_out, segment_ids[0])
    d_input = transposed_product(d_keyval, lax.all_gather(kv_weight, "shard", axis=0, tiled=True))
    columns = layer_input
    owned = lax.psum_scatter(
        lax.dot_general(
            columns, d_keyval, (((0,), (0,)), ((), ())), preferred_element_type=jnp.float32
        ).astype(jnp.bfloat16),
        "shard",
        scatter_dimension=0,
        tiled=True,
    ).astype(jnp.float32)
    d_kv_weight = lax.psum(owned, "rep")
    return (d_input.astype(jnp.bfloat16), d_queries, d_kv_weight)


def solution(mesh):
    return jax.shard_map(
        body,
        mesh=mesh,
        in_specs=(
            P(("rep", "shard"), None),
            P(("rep", "shard"), None),
            P(("rep", "shard"), None),
            P(("rep", "shard"), None),
            P("shard", None),
        ),
        out_specs=(P(("rep", "shard"), None), P(("rep", "shard"), None), P("shard", None)),
        check_vma=False,
    )
```

profile of v0, /device:TPU:0, one launch (start us, length us, event | category | flops | bytes accessed | tf_op | source)
XLA Modules:
  0.0 215.6 jit_solution(2832292008116182389)
XLA Ops:
  7.2 0.0 copy-start
  7.2 0.0 all-gather.2.cloned.1.call-start
  7.2 0.7 all-gather.2.cloned.1.call-update
  7.9 0.0 reduce-scatter.2.cloned.1.call-start
  8.0 1.0 copy.29
  9.0 1.0 copy.9
  10.0 0.8 fusion.17
  10.8 75.4 %all-gather.2.cloned.1.call-done = bf16[8192,256]{1,0:T(8,128)(2,1)} async-done(((bf16[1024,256]{1,0:T(8,128)(2,1)}), bf16[8192,256]{1,0:T(8,128)(2,1)}) %all-gather.2.cloned.1.call-update) | async-done | bytes 4194320 | tf_op jit(solution)/shard_map/all_gather | solution.py:48
  86.3 0.0 copy-done
  86.3 2.9 %convolution_convert_fusion.2 = bf16[128,256]{1,0:T(8,128)(2,1)S(1)} fusion(bf16[128,8192]{1,0:T(8,128)(2,1)S(1)} %copy-done, bf16[8192,256]{1,0:T(8,128)(2,1)} %all-gather.2.cloned.1.call-done), kind=kOutput, calls=%fused_computation.19 | convolution fusion | flops 536903680 | bytes 6356992 | tf_op jit(solution)/shard_map/dot_general | solution.py:46
  89.2 0.2 fusion.25
  89.4 0.2 fusion.12
  89.7 0.2 fusion.15
  89.9 0.2 fusion.10
  90.1 0.2 fusion.14
  90.3 3.2 %fusion.1 = bf16[8192,256]{0,1:T(8,128)(2,1)} fusion(bf16[128,8192]{1,0:T(8,128)(2,1)S(1)} %copy-done, bf16[128,128]{0,1:T(8,128)(2,1)S(1)} %fusion.15, bf16[128,128]{0,1:T(8,128)(2,1)S(1)} %fusion.14), kind=kOutput, calls=%fused_computation.2 | convolution fusion | flops 539099136 | bytes 6356992 | tf_op jit(solution)/shard_map/dot_general | solution.py:55
  93.5 0.0 reduce-scatter.2.cloned.1.call-update
  93.5 0.2 fusion.11
  93.7 0.8 copy.18
  94.5 5.0 %convolution_convert_fusion.1 = bf16[128,8192]{1,0:T(8,128)(2,1)} fusion(bf16[8192,256]{1,0:T(8,128)(2,1)} %all-gather.2.cloned.1.call-done, bf16[128,128]{0,1:T(8,128)(2,1)S(1)} %fusion.15, bf16[128,128]{0,1:T(8,128)(2,1)S(1)} %fusion.14), kind=kOutput, calls=%fused_computation.3 | convolution fusion | flops 538050560 | bytes 6356992 | tf_op jit(solution)/shard_map/dot_general | solution.py:39
  99.5 80.9 %reduce-scatter.2.cloned.1.call-done = bf16[1024,256]{0,1:T(8,128)(2,1)} async-done(((bf16[8192,256]{0,1:T(8,128)(2,1)}), bf16[1024,256]{0,1:T(8,128)(2,1)}) %reduce-scatter.2.cloned.1.call-update) | async-done | bytes 524304 | tf_op jit(solution)/shard_map/reduce_scatter | solution.py:54
  180.4 27.1 %all-reduce.1 = f32[1024,256]{0,1:T(8,128)S(1)} all-reduce(bf16[1024,256]{0,1:T(8,128)(2,1)} %reduce-scatter.2.cloned.1.call-done), channel_id=1, replica_groups=mesh['rep'=4,'shard'=8] {'rep'}, use_global_device_ids=true, to_apply=%region_4.5 | all-reduce | flops 262144 | bytes 1572864 | tf_op jit(solution)/shard_map/psum | solution.py:62
  207.4 1.3 copy.19
Async XLA Ops:
  7.2 79.1 %copy-start = (bf16[128,8192]{1,0:T(8,128)(2,1)S(1)}, bf16[128,8192]{1,0:T(8,128)(2,1)}, u32[]{:S(2)}) copy-start(bf16[128,8192]{1,0:T(8,128)(2,1)} %param.5) | copy-start | bytes 6291460
  7.2 79.1 %all-gather.2.cloned.1.call-start = ((), (), s32[]{:S(2)}) async-start(), calls=%async_computation.1 | async-start | bytes 4718592 | tf_op jit(solution)/shard_map/all_gather | solution.py:48
  7.9 172.5 %reduce-scatter.2.cloned.1.call-start = ((), (), s32[]{:S(2)}) async-start(), calls=%async_computation.2 | async-start | bytes 4718592 | tf_op jit(solution)/shard_map/reduce_scatter | solution.py:54
Sparse Core Ops, SparseCore 0:
  10.1 76.0 all-gather.1
  93.6 86.7 reduce-scatter.1
where the time goes:
time: 216 us
  waiting for transfers between devices  157 us (73%)
  blocking collectives  27.1 us (13%)
  between operations  14.1 us (7%)
  matrix products  12.4 us (6%)
  local copies, waits for them, and re-layouts  4.13 us (2%)
    reduce_scatter x1, waiting for transfers between devices, body(): lax.psum_scatter(lax.dot_general(columns, d_keyval, (((0,), (0,)), ((), (...  80.9 us
    all_gather x1, waiting for transfers between devices, body(): lax.all_gather(kv_weight, 'shard', axis=0, tiled=True)  75.4 us
    psum x1, blocking collectives, body(): d_kv_weight = lax.psum(owned, 'rep')  27.1 us
    dot_general x1, matrix products, transposed_product(): lax.dot_general(left, right, (((1,), (1,)), ((), ())), preferred_element_...  5.01 us
  transfers between devices with their start and end apart: 2, of which 2 were waited for; matrix products, arithmetic and copies ran while one was open for 4% of the time, Pallas kernels for 0%

commit v1 on v0

v1 whole, which is shorter than its diff:
```python
import functools

import jax
import jax.numpy as jnp
from jax import lax
from jax.experimental import pallas as pl
from jax.experimental.pallas import tpu as pltpu
from jax.sharding import PartitionSpec as P

HEAD = 128
QH = 4
SCALE = 1.0 / HEAD**0.5
NEAR = 2
FRONT = 30 * 10**9
SLIGHT = 5 * 10**9
F32 = jnp.float32
BF16 = jnp.bfloat16
VMEM = pl.BlockSpec(memory_space=pltpu.VMEM)
HBM = pl.BlockSpec(memory_space=pltpu.HBM)
ANY = pl.BlockSpec(memory_space=pl.ANY)
PARAMS = pltpu.CompilerParams(vmem_limit_bytes=24 * 1024 * 1024)


def dot(a, b, dims):
    return lax.dot_general(a, b, (dims, ((), ())), preferred_element_type=F32)


class Plan:
    def __init__(self, ranks, shards, rows, width, deep, cols):
        self.ranks, self.shards = ranks, shards
        self.rows, self.width, self.deep, self.cols = rows, width, deep, cols
        self.group = min(4, ranks, deep // 128)
        self.half = deep // 2
        self.part = deep // self.group
        self.far = shards - NEAR
        self.blocks = min(1, self.group - 2)
        self.near_width = NEAR * self.half
        self.far_width = self.far * self.part

    def sub(self, rank):
        return (rank // 2) % (self.group // 2)

    def half_at(self, shard, rank):
        return shard * self.deep + (rank % 2) * self.half

    def part_at(self, shard, rank):
        return self.half_at(shard, rank) + self.sub(rank) * self.part


def lanes(ref, start, size):
    if not isinstance(start, int):
        start = pl.multiple_of(start, 128)
    return ref.at[:, pl.ds(start, size)]


def launch(pairs, sems):
    copies = [pltpu.make_async_copy(a, b, sems.at[i]) for i, (a, b) in enumerate(pairs)]
    for copy in copies:
        copy.start()
    return copies


def finish(copies):
    for copy in copies:
        copy.wait()


def cut_kernel(plan, x, weight, half, part, *refs):
    outs, sems = refs[:-1], refs[-1]
    r, s = lax.axis_index("rep"), lax.axis_index("shard")
    begin = pl.multiple_of(plan.half_at(0, r), plan.half)
    inner = pl.multiple_of(plan.part_at(0, r), plan.part)
    pairs = [(weight.at[pl.ds(inner, plan.part)], part), (weight.at[pl.ds(begin, plan.half)], half)]
    for d in range(2, plan.group):
        block = outs[0].at[(d - 2) * plan.rows : (d - 1) * plan.rows]
        for e in range(plan.far):
            source = lanes(x, plan.part_at(s ^ (e + NEAR), r ^ d), plan.part)
            pairs.append((source, lanes(block, e * plan.part, plan.part)))
    finish(launch(pairs, sems))


def columns(plan, x, out, r, s):
    pairs = []
    for e in range(NEAR):
        source = lanes(x, plan.half_at(s ^ e, r), plan.half)
        pairs.append((source, lanes(out, e * plan.half, plan.half)))
    for e in range(plan.far):
        source = lanes(x, plan.part_at(s ^ (e + NEAR), r), plan.part)
        pairs.append((source, lanes(out, plan.near_width + e * plan.part, plan.part)))
    return pairs


def stage_kernel(plan, x, q, do, seg_col, seg_row, own, qs, dos, mask, partner, *refs):
    outs, sems = refs[:-1], refs[-1]
    rows = plan.rows
    r, s = lax.axis_index("rep"), lax.axis_index("shard")
    pairs = columns(plan, x, partner, r ^ 1, s)
    for d in range(2, plan.group):
        for e in range(NEAR):
            source = lanes(x, plan.part_at(s ^ e, r ^ d), plan.part)
            pairs.append((source, lanes(outs[d - 2], e * plan.part, plan.part)))
    pairs += columns(plan, x, own, r, s)
    for h in range(QH):
        pairs.append((lanes(q, h * HEAD, HEAD), qs.at[h * rows : (h + 1) * rows]))
        pairs.append((lanes(do, h * HEAD, HEAD), dos.at[h * rows : (h + 1) * rows]))
    copies = launch(pairs, sems)
    to = lax.broadcasted_iota(jnp.int32, (rows, rows), 0)
    of = lax.broadcasted_iota(jnp.int32, (rows, rows), 1)
    allowed = (seg_col[...] == seg_row[...]) & (of <= to)
    mask[...] = allowed.astype(F32)
    finish(copies)


def project_kernel(plan, own, partner, *refs):
    rows, half, part = plan.rows, plan.half, plan.part
    crossed, refs = refs[: plan.blocks], refs[plan.blocks :]
    near, refs = refs[:NEAR], refs[NEAR:]
    far, outs = refs[: plan.far], refs[plan.far :]
    both = jnp.zeros((2 * rows, plan.cols), F32)
    for e in range(NEAR):
        span = slice(e * half, (e + 1) * half)
        left = jnp.concatenate([own[:, span], partner[:, span]], axis=0)
        both += dot(left, near[e][...], ((1,), (0,)))
    wide = jnp.zeros(((2 + plan.blocks) * rows, plan.cols), F32)
    for e in range(plan.far):
        span = slice(e * part, (e + 1) * part)
        shifted = slice(plan.near_width + e * part, plan.near_width + (e + 1) * part)
        left = [own[:, shifted], partner[:, shifted]] + [o[:rows, span] for o in crossed]
        wide += dot(jnp.concatenate(left, axis=0), far[e][...], ((1,), (0,)))
    outs[0][...] = both[:rows] + wide[:rows]
    outs[1][...] = (both[rows:] + wide[rows : 2 * rows]).astype(BF16)
    for out in outs[2:]:
        out[...] = wide[2 * rows :].astype(BF16)


def project_last_kernel(plan, after, handed, *refs):
    far, out = refs[: plan.far], refs[-1]
    wide = jnp.zeros(out.shape, F32)
    for e in range(plan.far):
        left = handed[:, e * plan.part : (e + 1) * plan.part]
        wide += dot(left, far[e][...], ((1,), (0,)))
    out[...] = wide.astype(BF16)


def attention_kernel(group, qs_ref, dos_ref, mask, *refs):
    terms, (dq, dkv) = refs[:group], refs[-2:]
    rows = mask.shape[0]
    keyval = terms[0][...]
    for term in terms[1:]:
        keyval += term[...].astype(F32)
    keys = keyval[:, :HEAD].astype(BF16)
    values = keyval[:, HEAD:].astype(BF16)
    allowed = jnp.concatenate([mask[...]] * QH, axis=0) > 0.5
    qs, dos = qs_ref[...], dos_ref[...]
    scores = dot(qs, keys, ((1,), (1,))) * SCALE
    dprob = dot(dos, values, ((1,), (1,)))
    scores = jnp.where(allowed, scores, -1e30)
    top = jnp.max(scores, axis=1, keepdims=True)
    weights = jnp.where(allowed, jnp.exp(scores - top), 0.0)
    probs = weights / jnp.sum(weights, axis=1, keepdims=True)
    low = probs.astype(BF16)
    delta = jnp.sum(low.astype(F32) * dprob, axis=1, keepdims=True)
    dscore = (probs * (dprob - delta)).astype(BF16)
    d_keys = dot(dscore, qs, ((0,), (0,)))
    d_values = dot(low, dos, ((0,), (0,)))
    dkv[:, :HEAD] = (d_keys * SCALE).astype(BF16)
    dkv[:, HEAD:] = d_values.astype(BF16)
    d_queries = (dot(dscore, keys, ((1,), (0,))) * SCALE).astype(BF16)
    for h in range(QH):
        dq[:, h * HEAD : (h + 1) * HEAD] = d_queries[h * rows : (h + 1) * rows]


def weight_grad_kernel(plan, shards, own, partner, *refs):
    group, rows, part, half = plan.group, plan.rows, plan.part, plan.half
    others, refs = refs[: group - 2], refs[group - 2 :]
    grads, outs = refs[:group], refs[group:]
    r = lax.axis_index("rep")
    grad = jnp.concatenate([g[...] for g in grads], axis=0)
    inner = plan.sub(r) * part
    for e, (index, row) in shards.items():
        if e < NEAR:
            at = pl.multiple_of(e * half + inner, 128)
            span = slice(e * part, (e + 1) * part)
            left = [own[:, pl.ds(at, part)], partner[:, pl.ds(at, part)]]
        else:
            start = (e - NEAR) * part
            span = slice(start, start + part)
            shifted = slice(plan.near_width + start, plan.near_width + start + part)
            left = [own[:, shifted], partner[:, shifted]]
        left += [o[:rows, span] for o in others]
        term = dot(jnp.concatenate(left, axis=0), grad, ((0,), (0,))).astype(BF16)
        outs[index][row * part : (row + 1) * part] = term


def gather_kernel(plan, after, *refs):
    far, out = refs[: plan.far], refs[plan.far]
    for e in range(plan.far):
        out[e * plan.part : (e + 1) * plan.part] = far[e][...]


def input_grad_kernel(plan, after, grad, other, *refs):
    rows, half, part = plan.rows, plan.half, plan.part
    near, refs = refs[:NEAR], refs[NEAR:]
    far, outs = refs[: 1 + plan.blocks], refs[1 + plan.blocks :]
    r = lax.axis_index("rep")
    both = jnp.concatenate([grad[...], other[...]], axis=0)
    for e in range(NEAR):
        span = slice(e * half, (e + 1) * half)
        term = dot(both, near[e][...], ((1,), (1,))).astype(BF16)
        outs[0][:, span] = term[:rows]
        outs[1][:, span] = term[rows:]
    for e in range(plan.far):
        for i, piece in enumerate(far):
            sub = plan.sub(r) if i == 0 else 1 - plan.sub(r)
            at = pl.multiple_of((NEAR + e) * half + sub * part, 128)
            term = dot(both, piece[e * part : (e + 1) * part], ((1,), (1,))).astype(BF16)
            outs[0][:, pl.ds(at, part)] = term[:rows]
            outs[1][:, pl.ds(at, part)] = term[rows:]


def place_kernel(plan, mine, came, out, sems):
    r, s = lax.axis_index("rep"), lax.axis_index("shard")
    pairs = []
    for d, ref in enumerate((mine, came)):
        for e in range(plan.shards):
            target = lanes(out, plan.half_at(s ^ e, r ^ d), plan.half)
            pairs.append((lanes(ref, e * plan.half, plan.half), target))
    finish(launch(pairs, sems))


def pair_kernel(mine, came, out):
    out[...] = (mine[...].astype(F32) + came[...].astype(F32)).astype(BF16)


def near_kernel(mine, other, came, keep, send):
    rows = mine.shape[0]
    keep[...] = mine[...].astype(F32) + came[:rows].astype(F32)
    send[...] = (other[...].astype(F32) + came[rows:].astype(F32)).astype(BF16)


def total_kernel(mine, *refs):
    total = mine[...].astype(F32)
    for ref in refs[:-1]:
        total += ref[...].astype(F32)
    refs[-1][...] = total.astype(refs[-1].dtype)


def rows_kernel(plan, flips, *refs):
    terms, (out, wide, sems) = refs[-3 - len(flips) : -3], refs[-3:]
    r = lax.axis_index("rep")
    pairs = []
    for i, (flip, term) in enumerate(zip(flips, terms)):
        wide[i * plan.part : (i + 1) * plan.part] = term[...].astype(F32)
        start = pl.multiple_of(plan.part_at(0, r ^ flip), plan.part)
        pairs.append((wide.at[i * plan.part : (i + 1) * plan.part], out.at[pl.ds(start, plan.part)]))
    finish(launch(pairs, sems))


def hand_on_kernel(after, block, out):
    rows = out.shape[0]
    out[...] = block[rows:]


def nothing(*refs):
    pass


def gate(array, *waits, weight=0, spec=ANY):
    operand = pltpu.with_memory_space_constraint(array, pltpu.VMEM)
    if spec is HBM:
        waits = [pltpu.with_memory_space_constraint(wait, pltpu.HBM) for wait in waits]
    return pl.pallas_call(
        nothing,
        out_shape=pltpu.VMEM(array.shape, array.dtype),
        in_specs=[VMEM] + [spec] * len(waits),
        out_specs=VMEM,
        input_output_aliases={0: 0},
        compiler_params=PARAMS,
        cost_estimate=pl.CostEstimate(flops=weight, bytes_accessed=0, transcendentals=0),
        name="gate",
    )(operand, *waits)


def call(kernel, name, ins, in_specs, shapes, out_spec, scratch=(), copies=0, loose=0, weight=0, alias=()):
    sems = [pltpu.SemaphoreType.DMA((copies,))] if copies else []
    spaces = {id(HBM): pltpu.HBM, id(VMEM): pltpu.VMEM}
    ins = [
        pltpu.with_memory_space_constraint(a, spaces[id(spec)]) if id(spec) in spaces else a
        for a, spec in zip(ins, in_specs)
    ]
    shapes = [pltpu.VMEM(a.shape, a.dtype) if i >= loose else a for i, a in enumerate(shapes)]
    return pl.pallas_call(
        kernel,
        out_shape=tuple(shapes),
        in_specs=in_specs,
        out_specs=tuple([out_spec] * len(shapes)),
        scratch_shapes=list(scratch) + sems,
        input_output_aliases=dict(alias),
        compiler_params=PARAMS,
        cost_estimate=pl.CostEstimate(flops=weight, bytes_accessed=0, transcendentals=0),
        name=name,
    )(*ins)


def body(ranks, shards, layer_input, queries, d_out, segment_ids, kv_weight):
    rows, width = layer_input.shape
    deep, cols = kv_weight.shape
    plan = Plan(ranks, shards, rows, width, deep, cols)
    group, half, part = plan.group, plan.half, plan.part
    lines = shards // 2
    r = lax.axis_index("rep")
    shape = jax.ShapeDtypeStruct

    def swap(array, axis, flip):
        size = ranks if axis == "rep" else shards
        return lax.ppermute(array, axis, [(i, i ^ flip) for i in range(size)])

    full = shape((rows, plan.near_width + plan.far_width), BF16)
    others = group - 2
    blocks = plan.blocks
    cuts = call(
        functools.partial(cut_kernel, plan), "cut", [layer_input, kv_weight], [HBM] * 2,
        [shape((half, cols), BF16), shape((part, cols), BF16)]
        + [shape((others * rows, plan.far_width), BF16)] * blocks,
        VMEM, copies=2 + others * plan.far,
    )
    own_half, own_part = cuts[:2]

    def hand_on(block, after, weight):
        half_block = shape((rows, block.shape[1]), BF16)
        mine = call(
            hand_on_kernel, "hand_on", [after, block], [ANY, VMEM], [half_block], VMEM, weight=weight
        )[0]
        return [block, swap(mine, "rep", 1)]

    def write(flips, terms, given=(), waits=()):
        return call(
            functools.partial(rows_kernel, plan, flips), "rows", [*given, *waits, *terms],
            [HBM] * len(given) + [ANY] * len(waits) + [VMEM] * len(terms),
            [shape((deep, cols), F32)], HBM,
            scratch=[pltpu.VMEM((len(flips) * part, cols), F32)], copies=len(flips), loose=1,
            alias={0: 0} if given else {},
        )[0]

    def cross(pieces, *waits):
        return [swap(gate(p, *waits) if waits else p, "rep", 2) for p in pieces]

    far_cross = cross(cuts[2:])
    beside = swap(own_half, "shard", 1)
    ahead = swap(own_part, "shard", 2)
    apart = [swap(own_part, "shard", 2 * d) for d in range(2, lines)]
    near = [own_half, beside]
    far = [a for piece in (ahead, *apart) for a in (piece, swap(piece, "shard", 1))]
    corner = far[1]
    far_x = []
    for block in far_cross:
        far_x += hand_on(block, corner, FRONT)

    stacked = shape((QH * rows, HEAD), BF16)
    staged = call(
        functools.partial(stage_kernel, plan), "stage",
        [layer_input, queries, d_out, segment_ids.reshape(rows, 1), segment_ids],
        [HBM] * 3 + [VMEM] * 2,
        [full, stacked, stacked, shape((rows, rows), F32), full]
        + [shape((rows, NEAR * part), BF16)] * others,
        VMEM, copies=2 * shards + others * NEAR + 2 * QH, weight=SLIGHT,
    )
    own, qs, dos, mask = staged[:4]
    partner = swap(gate(staged[4], apart[0], corner, beside), "rep", 1)

    low = shape((rows, cols), BF16)
    terms = list(call(
        functools.partial(project_kernel, plan), "project",
        [own, partner, *far_x[:1], *near, *far], [VMEM] * (2 + blocks + NEAR + plan.far),
        [shape((rows, cols), F32)] + [low] * (1 + blocks), VMEM, weight=FRONT,
    ))
    for handed in far_x[1:]:
        terms += call(
            functools.partial(project_last_kernel, plan), "project_last",
            [terms[0], handed, *far], [ANY] + [VMEM] * (1 + plan.far), [low], VMEM,
        )
    terms = [terms[0]] + [swap(terms[d], "rep", d) for d in range(1, group)]

    d_queries, d_keyval = call(
        functools.partial(attention_kernel, group), "attention",
        [qs, dos, mask, *terms], [VMEM] * (3 + group),
        [shape(queries.shape, BF16), shape((rows, cols), BF16)], VMEM, loose=1, weight=FRONT,
    )

    grads = [d_keyval] + [swap(d_keyval, "rep", d) for d in range(1, group)]
    block = shape((part, cols), BF16)
    places = {2: (0, 0), 3: (0, 1), **{e: (e - 3, 0) for e in range(4, shards)}}
    outs = [shape((2 * part, cols), BF16)] + [block] * (shards - 4)
    sums = list(call(
        functools.partial(weight_grad_kernel, plan, places), "weight_grad",
        [own, partner, *far_x, *grads], [VMEM] * (2 * group), outs, VMEM,
    ))
    mine = call(
        functools.partial(gather_kernel, plan), "gather", [sums[0], *far], [ANY] + [VMEM] * plan.far,
        [shape((plan.far * part, cols), BF16)], VMEM,
    )
    far_rows_all = [*mine, *cross(list(mine) * blocks)]
    near_x = [swap(gate(a, d_keyval), "rep", d + 2) for d, a in enumerate(staged[5:])]
    held = []

    beyond = swap(gate(sums[0], *near_x[:1]), "shard", 2)

    def pair(d):
        came = swap(sums[places[2 * d + 1][0]], "shard", 1)
        mine = gate(sums[places[2 * d][0]], *held[-1:], weight=FRONT)
        out = call(pair_kernel, "pair", [mine, came], [VMEM] * 2, [block], VMEM)[0]
        held.append(out)
        return out

    pairs = {d: pair(d) for d in range(2, lines)}
    total = [swap(pairs[d], "shard", 2 * d) for d in range(2, lines)]
    near_terms = call(
        functools.partial(weight_grad_kernel, plan, {0: (0, 0), 1: (1, 0)}), "weight_grad_near",
        [own, partner, *near_x, *grads], [VMEM] * (2 * group), [block] * 2, VMEM,
    )
    keep, send = call(
        near_kernel, "near", [*near_terms, beyond], [VMEM] * 3, [shape((part, cols), F32), block], VMEM
    )
    total.append(swap(gate(send, pairs[lines - 1]), "shard", 1))
    again = ranks > group
    quarter = call(
        total_kernel, "total", [keep, *total], [VMEM] * (1 + len(total)),
        [shape((part, cols), F32 if again else BF16)], VMEM,
    )[0]
    if again:
        rings = [[g + group * k for k in range(ranks // group)] for g in range(group)]
        quarter = lax.psum(quarter, "rep", axis_index_groups=rings).astype(BF16)
    halves = shape((rows, shards * half), BF16)
    backs = call(
        functools.partial(input_grad_kernel, plan), "input_grad",
        [quarter, *grads[:2], *near, *far_rows_all], [ANY] + [VMEM] * (3 + NEAR + blocks),
        [halves] * 2, VMEM,
    )
    backs = [backs[0], swap(backs[1], "rep", 1)]
    quarters = [quarter, swap(quarter, "rep", 1)]
    d_kv_weight = write(range(2), quarters, waits=backs[:1])
    for crossing in cross([quarter] * blocks):
        crossing = gate(crossing, d_kv_weight, weight=FRONT, spec=HBM)
        quarters += [crossing, swap(crossing, "rep", 1)]
    d_input = call(
        functools.partial(place_kernel, plan), "place", backs, [VMEM] * 2,
        [shape((rows, width), BF16)], HBM, copies=2 * shards, loose=1, weight=FRONT,
    )[0]
    if group > 2:
        d_kv_weight = write(range(2, group), quarters[2:], [d_kv_weight, d_input])
    return (d_input, d_queries, d_kv_weight)


def solution(mesh):
    ranks, shards = mesh.shape["rep"], mesh.shape["shard"]
    spread = P(("rep", "shard"), None)
    return jax.shard_map(
        functools.partial(body, ranks, shards),
        mesh=mesh,
        in_specs=(spread, spread, spread, spread, P("shard", None)),
        out_specs=(spread, spread, P("shard", None)),
        check_vma=False,
    )
```

time: 216 us -> 67.7 us (0.31)
  waiting for transfers between devices: 157 us -> 26.9 us
  starting transfers between devices: 0.08 us -> 29.2 us
  blocking collectives: 27.1 us -> 0 us
  between operations: 14.1 us -> 0.81 us
  matrix products: 12.4 us -> 0 us
  Pallas kernels: 0 us -> 10.5 us
  local copies, waits for them, and re-layouts: 4.13 us -> 0.12 us
    reduce_scatter x1 -> x0, waiting for transfers between devices: 80.9 us -> none  [body(): lax.psum_scatter(lax.dot_general(columns, d_keyval, (((0,), (0,)), ((), (...]
    all_gather x1 -> x0, waiting for transfers between devices: 75.4 us -> none  [body(): lax.all_gather(kv_weight, 'shard', axis=0, tiled=True)]
    ppermute x0 -> x29, starting transfers between devices: none -> 29.2 us  [swap(): return lax.ppermute(array, axis, [(i, i ^ flip) for i in range(size)])]
    psum x1 -> x0, blocking collectives: 27.1 us -> none  [body(): d_kv_weight = lax.psum(owned, 'rep')]
    ppermute x0 -> x29, waiting for transfers between devices: none -> 26.9 us  [swap(): return lax.ppermute(array, axis, [(i, i ^ flip) for i in range(size)])]
    dot_general x8 -> x0, matrix products: 12.1 us -> none  [the longest x1 5.01 us: transposed_product(): lax.dot_general(left, right, (((1,), (1,)), ((), ())), preferred_element_...]
    pallas_call x0 -> x25, Pallas kernels: none -> 10.5 us  [the longest x17 10.5 us: call(): pl.pallas_call(kernel, out_shape=tuple(shapes), in_specs=in_specs, out_sp...]
    unnamed x5 -> x2, local copies, waits for them, and re-layouts: 3.11 us -> 0.01 us
  transfers between devices with their start and end apart: 2 -> 29, of which waited for: 2 -> 18; matrix products, arithmetic and copies ran while one was open for 4% -> 0% of each run, Pallas kernels for 0% -> 10%
where the time goes in v1:
time: 67.7 us; the launch traced here: 67.6 us
  starting transfers between devices  29.2 us (43%)
  waiting for transfers between devices  26.9 us (40%)
  Pallas kernels  10.5 us (16%)
  between operations  0.81 us (1%)
    ppermute x29, starting transfers between devices, swap(): return lax.ppermute(array, axis, [(i, i ^ flip) for i in range(size)])  29.2 us
    ppermute x29, waiting for transfers between devices, swap(): return lax.ppermute(array, axis, [(i, i ^ flip) for i in range(size)])  26.9 us
    pallas_call x17, Pallas kernels, call(): pl.pallas_call(kernel, out_shape=tuple(shapes), in_specs=in_specs, out_sp...  10.5 us
  transfers between devices with their start and end apart: 29, of which 18 were waited for; matrix products, arithmetic and copies ran while one was open for 0% of the time, Pallas kernels for 10%

profile of v1, /device:TPU:0, one launch (start us, length us, event | category | flops | bytes accessed | tf_op | source)
XLA Modules:
  0.0 67.6 jit_solution(11725516707256545766)
XLA Ops:
  0.6 1.4 %cut.1 = (bf16[512,256]{1,0:T(8,128)(2,1)S(1)}, bf16[256,256]{1,0:T(8,128)(2,1)S(1)}, bf16[256,1536]{1,0:T(8,128)(2,1)S(1)}) custom-call(bf16[128,8192]{1,0:T(8,128)(2,1)} %x.3, bf16[1024,256]{1,0:T(8,128)(2,1)} %weight.1), custom_call_target="tpu_custom_call" | custom-call | tf_op jit(solution)/shard_map/cut/pallas_call | solution.py:292
  2.0 3.0 %collective-permute-start.5 = (bf16[256,1536]{1,0:T(8,128)(2,1)S(1)}, bf16[256,1536]{1,0:T(8,128)(2,1)S(1)}, u32[]{:S(2)}, u32[]{:S(2)}) collective-permute-start(bf16[256,1536]{1,0:T(8,128)(2,1)S(1)} %get-tuple-element.37), channel_id=1, source_target_pairs={{0,16},{8,24},{16,0},{24,8},{1,17},{9,25},{17,1},{25,9},{2,18},{10... | collective-permute-start | bytes 2359304 | tf_op jit(solution)/shard_map/ppermute | solution.py:316
  5.0 1.6 %collective-permute-start.1 = (bf16[256,256]{1,0:T(8,128)(2,1)S(1)}, bf16[256,256]{1,0:T(8,128)(2,1)S(1)}, u32[]{:S(2)}, u32[]{:S(2)}) collective-permute-start(bf16[256,256]{1,0:T(8,128)(2,1)S(1)} %get-tuple-element.31), channel_id=1, source_target_pairs={{0,2},{1,3},{2,0},{3,1},{4,6},{5,7},{6,4},{7,5},{8,10},{9,11},{10,... | collective-permute-start | bytes 393224 | tf_op jit(solution)/shard_map/ppermute | solution.py:316
  6.6 2.6 %collective-permute-start = (bf16[256,256]{1,0:T(8,128)(2,1)S(1)}, bf16[256,256]{1,0:T(8,128)(2,1)S(1)}, u32[]{:S(2)}, u32[]{:S(2)}) collective-permute-start(bf16[256,256]{1,0:T(8,128)(2,1)S(1)} %get-tuple-element.31), channel_id=1, source_target_pairs={{0,4},{1,5},{2,6},{3,7},{4,0},{5,1},{6,2},{7,3},{8,12},{9,13},{10,... | collective-permute-start | bytes 393224 | tf_op jit(solution)/shard_map/ppermute | solution.py:316
  9.4 1.5 %collective-permute-start.3 = (bf16[512,256]{1,0:T(8,128)(2,1)S(1)}, bf16[512,256]{1,0:T(8,128)(2,1)S(1)}, u32[]{:S(2)}, u32[]{:S(2)}) collective-permute-start(bf16[512,256]{1,0:T(8,128)(2,1)S(1)} %get-tuple-element.32.refs_1_.refs_0_), channel_id=1, source_target_pairs={{0,1},{1,0},{2,3},{3,2},{4,5},{5,4},{6,7},{7,6},{8,9},{9,8},{10,11... | collective-permute-start | bytes 786440 | tf_op jit(solution)/shard_map/ppermute | solution.py:316
  11.5 1.5 %collective-permute-start.2 = (bf16[256,256]{1,0:T(8,128)(2,1)S(1)}, bf16[256,256]{1,0:T(8,128)(2,1)S(1)}, u32[]{:S(2)}, u32[]{:S(2)}) collective-permute-start(bf16[256,256]{1,0:T(8,128)(2,1)S(1)} %collective-permute-done.1.refs_3_.refs_0_), channel_id=1, source_target_pairs={{0,1},{1,0},{2,3},{3,2},{4,5},{5,4},{6,7},{7,6},{8,9},{9,8},{10,11... | collective-permute-start | bytes 393224 | tf_op jit(solution)/shard_map/ppermute | solution.py:316
  13.0 1.7 %stage.1 = (bf16[128,2560]{1,0:T(8,128)(2,1)S(1)}, bf16[512,128]{1,0:T(8,128)(2,1)S(1)}, bf16[512,128]{1,0:T(8,128)(2,1)S(1)}, f32[128,128]{1,0:T(8,128)S(1)}, b...) custom-call(bf16[128,8192]{1,0:T(8,128)(2,1)} %x.3, bf16[128,512]{1,0:T(8,128)(2,1)} %q.1, ...), custom_call_target="tpu_custom_call" | custom-call | flops 5000000000 | tf_op jit(solution)/shard_map/stage/pallas_call | solution.py:292
  14.7 4.6 %collective-permute-done.refs_1_.refs_5_.refs_2_ = bf16[256,256]{1,0:T(8,128)(2,1)S(1)} collective-permute-done((bf16[256,256]{1,0:T(8,128)(2,1)S(1)}, bf16[256,256]{1,0:T(8,128)(2,1)S(1)}, u32[]{:S(2)}, u32[]{:S(2)}) %collective-permute-start) | collective-permute-done | bytes 131104 | tf_op jit(solution)/shard_map/ppermute | solution.py:316
  19.3 1.5 %collective-permute-start.6 = (bf16[256,256]{1,0:T(8,128)(2,1)S(1)}, bf16[256,256]{1,0:T(8,128)(2,1)S(1)}, u32[]{:S(2)}, u32[]{:S(2)}) collective-permute-start(bf16[256,256]{1,0:T(8,128)(2,1)S(1)} %collective-permute-done.refs_1_.refs_5_.refs_2_), channel_id=1, source_target_pairs={{0,1},{1,0},{2,3},{3,2},{4,5},{5,4},{6,7},{7,6},{8,9},{9,8},{10,11... | collective-permute-start | bytes 393224 | tf_op jit(solution)/shard_map/ppermute | solution.py:316
  21.5 1.1 %collective-permute-done.5.refs_0_.block = bf16[256,1536]{1,0:T(8,128)(2,1)S(1)} collective-permute-done((bf16[256,1536]{1,0:T(8,128)(2,1)S(1)}, bf16[256,1536]{1,0:T(8,128)(2,1)S(1)}, u32[]{:S(2)}, u32[]{:S(2)}) %collective-permute-start.5) | collective-permute-done | bytes 786464 | tf_op jit(solution)/shard_map/ppermute | solution.py:316
  22.7 1.5 %collective-permute-done.6.refs_6_.refs_3_ = bf16[256,256]{1,0:T(8,128)(2,1)S(1)} collective-permute-done((bf16[256,256]{1,0:T(8,128)(2,1)S(1)}, bf16[256,256]{1,0:T(8,128)(2,1)S(1)}, u32[]{:S(2)}, u32[]{:S(2)}) %collective-permute-start.6) | collective-permute-done | bytes 131104 | tf_op jit(solution)/shard_map/ppermute | solution.py:316
  24.2 1.5 %collective-permute-done.8.refs_8_.refs_5_ = bf16[256,256]{1,0:T(8,128)(2,1)S(1)} collective-permute-done((bf16[256,256]{1,0:T(8,128)(2,1)S(1)}, bf16[256,256]{1,0:T(8,128)(2,1)S(1)}, u32[]{:S(2)}, u32[]{:S(2)}) %collective-permute-start.8) | collective-permute-done | bytes 131104 | tf_op jit(solution)/shard_map/ppermute | solution.py:316
  27.3 1.3 %collective-permute-start.12 = (bf16[128,256]{1,0:T(8,128)(2,1)S(1)}, bf16[128,256]{1,0:T(8,128)(2,1)S(1)}, u32[]{:S(2)}, u32[]{:S(2)}) collective-permute-start(bf16[128,256]{1,0:T(8,128)(2,1)S(1)} %project_last.1), channel_id=1, source_target_pairs={{0,24},{8,16},{16,8},{24,0},{1,25},{9,17},{17,9},{25,1},{2,26},{10... | collective-permute-start | bytes 196616 | tf_op jit(solution)/shard_map/ppermute | solution.py:316
  28.7 2.7 %collective-permute-done.10.refs_2_ = bf16[128,256]{1,0:T(8,128)(2,1)S(1)} collective-permute-done((bf16[128,256]{1,0:T(8,128)(2,1)S(1)}, bf16[128,256]{1,0:T(8,128)(2,1)S(1)}, u32[]{:S(2)}, u32[]{:S(2)}) %collective-permute-start.10) | collective-permute-done | bytes 65568 | tf_op jit(solution)/shard_map/ppermute | solution.py:316
  31.9 1.4 %attention.1 = (bf16[128,512]{1,0:T(8,128)(2,1)}, bf16[128,256]{1,0:T(8,128)(2,1)S(1)}) custom-call(bf16[512,128]{1,0:T(8,128)(2,1)S(1)} %get-tuple-element.34.qs_ref, bf16[512,128]{1,0:T(8,128)(2,1)S(1)} %get-tuple-element.35.dos_ref, f32[128,128]{1,0:T(8,128)S(1)} %get-tuple-element.36.mask, f32[128,256]{1,0:T(8,128)S(1)} %get-tuple-element.38.after.refs_0_, ...), custom_call_target="tpu_custom_call" | custom-call | flops 30000001024 | tf_op jit(solution)/shard_map/attention/pallas_call | solution.py:292
  33.6 0.9 %collective-permute-start.16 = (bf16[128,256]{1,0:T(8,128)(2,1)S(1)}, bf16[128,256]{1,0:T(8,128)(2,1)S(1)}, u32[]{:S(2)}, u32[]{:S(2)}) collective-permute-start(bf16[128,256]{1,0:T(8,128)(2,1)S(1)} %get-tuple-element.41.refs_1_.refs_2_.grad), channel_id=1, source_target_pairs={{0,16},{8,24},{16,0},{24,8},{1,17},{9,25},{17,1},{25,9},{2,18},{10... | collective-permute-start | bytes 196616 | tf_op jit(solution)/shard_map/ppermute | solution.py:316
  35.2 1.0 %collective-permute-start.13 = (bf16[128,512]{1,0:T(8,128)(2,1)S(1)}, bf16[128,512]{1,0:T(8,128)(2,1)S(1)}, u32[]{:S(2)}, u32[]{:S(2)}) collective-permute-start(bf16[128,512]{1,0:T(8,128)(2,1)S(1)} %gate.9), channel_id=1, source_target_pairs={{0,16},{8,24},{16,0},{24,8},{1,17},{9,25},{17,1},{25,9},{2,18},{10... | collective-permute-start | bytes 393224 | tf_op jit(solution)/shard_map/ppermute | solution.py:316
  37.1 1.1 %collective-permute-done.16.refs_4_ = bf16[128,256]{1,0:T(8,128)(2,1)S(1)} collective-permute-done((bf16[128,256]{1,0:T(8,128)(2,1)S(1)}, bf16[128,256]{1,0:T(8,128)(2,1)S(1)}, u32[]{:S(2)}, u32[]{:S(2)}) %collective-permute-start.16) | collective-permute-done | bytes 65568 | tf_op jit(solution)/shard_map/ppermute | solution.py:316
  39.6 1.5 %collective-permute-start.19 = (bf16[256,256]{1,0:T(8,128)(2,1)S(1)}, bf16[256,256]{1,0:T(8,128)(2,1)S(1)}, u32[]{:S(2)}, u32[]{:S(2)}) collective-permute-start(bf16[256,256]{1,0:T(8,128)(2,1)S(1)} %get-tuple-element.48), channel_id=1, source_target_pairs={{0,1},{1,0},{2,3},{3,2},{4,5},{5,4},{6,7},{7,6},{8,9},{9,8},{10,11... | collective-permute-start | bytes 393224 | tf_op jit(solution)/shard_map/ppermute | solution.py:316
  41.7 1.1 %collective-permute-start.24 = (bf16[1536,256]{1,0:T(8,128)(2,1)S(1)}, bf16[1536,256]{1,0:T(8,128)(2,1)S(1)}, u32[]{:S(2)}, u32[]{:S(2)}) collective-permute-start(bf16[1536,256]{1,0:T(8,128)(2,1)S(1)} %gather.1.refs_2_), channel_id=1, source_target_pairs={{0,16},{8,24},{16,0},{24,8},{1,17},{9,25},{17,1},{25,9},{2,18},{10... | collective-permute-start | bytes 2359304 | tf_op jit(solution)/shard_map/ppermute | solution.py:316
  42.8 0.9 %collective-permute-start.18 = (bf16[512,256]{1,0:T(8,128)(2,1)S(1)}, bf16[512,256]{1,0:T(8,128)(2,1)S(1)}, u32[]{:S(2)}, u32[]{:S(2)}) collective-permute-start(bf16[512,256]{1,0:T(8,128)(2,1)S(1)} %gate.11), channel_id=1, source_target_pairs={{0,2},{1,3},{2,0},{3,1},{4,6},{5,7},{6,4},{7,5},{8,10},{9,11},{10,... | collective-permute-start | bytes 786440 | tf_op jit(solution)/shard_map/ppermute | solution.py:316
  44.9 1.0 %collective-permute-done.19.came = bf16[256,256]{1,0:T(8,128)(2,1)S(1)} collective-permute-done((bf16[256,256]{1,0:T(8,128)(2,1)S(1)}, bf16[256,256]{1,0:T(8,128)(2,1)S(1)}, u32[]{:S(2)}, u32[]{:S(2)}) %collective-permute-start.19) | collective-permute-done | bytes 131104 | tf_op jit(solution)/shard_map/ppermute | solution.py:316
  46.0 1.5 %collective-permute-start.20 = (bf16[256,256]{1,0:T(8,128)(2,1)S(1)}, bf16[256,256]{1,0:T(8,128)(2,1)S(1)}, u32[]{:S(2)}, u32[]{:S(2)}) collective-permute-start(bf16[256,256]{1,0:T(8,128)(2,1)S(1)} %pair.2.refs_1_), channel_id=1, source_target_pairs={{0,4},{1,5},{2,6},{3,7},{4,0},{5,1},{6,2},{7,3},{8,12},{9,13},{10,... | collective-permute-start | bytes 393224 | tf_op jit(solution)/shard_map/ppermute | solution.py:316
  47.5 0.9 %collective-permute-done.21.came = bf16[256,256]{1,0:T(8,128)(2,1)S(1)} collective-permute-done((bf16[256,256]{1,0:T(8,128)(2,1)S(1)}, bf16[256,256]{1,0:T(8,128)(2,1)S(1)}, u32[]{:S(2)}, u32[]{:S(2)}) %collective-permute-start.21) | collective-permute-done | bytes 131104 | tf_op jit(solution)/shard_map/ppermute | solution.py:316
  48.4 2.7 %collective-permute-start.22 = (bf16[256,256]{1,0:T(8,128)(2,1)S(1)}, bf16[256,256]{1,0:T(8,128)(2,1)S(1)}, u32[]{:S(2)}, u32[]{:S(2)}) collective-permute-start(bf16[256,256]{1,0:T(8,128)(2,1)S(1)} %pair.3.refs_1_), channel_id=1, source_target_pairs={{0,6},{1,7},{2,4},{3,5},{4,2},{5,3},{6,0},{7,1},{8,14},{9,15},{10,... | collective-permute-start | bytes 393224 | tf_op jit(solution)/shard_map/ppermute | solution.py:316
  51.1 1.4 %collective-permute-done.18.came = bf16[512,256]{1,0:T(8,128)(2,1)S(1)} collective-permute-done((bf16[512,256]{1,0:T(8,128)(2,1)S(1)}, bf16[512,256]{1,0:T(8,128)(2,1)S(1)}, u32[]{:S(2)}, u32[]{:S(2)}) %collective-permute-start.18) | collective-permute-done | bytes 262176 | tf_op jit(solution)/shard_map/ppermute | solution.py:316
  52.6 1.5 %collective-permute-start.23 = (bf16[256,256]{1,0:T(8,128)(2,1)S(1)}, bf16[256,256]{1,0:T(8,128)(2,1)S(1)}, u32[]{:S(2)}, u32[]{:S(2)}) collective-permute-start(bf16[256,256]{1,0:T(8,128)(2,1)S(1)} %gate.14), channel_id=1, source_target_pairs={{0,1},{1,0},{2,3},{3,2},{4,5},{5,4},{6,7},{7,6},{8,9},{9,8},{10,11... | collective-permute-start | bytes 393224 | tf_op jit(solution)/shard_map/ppermute | solution.py:316
  54.1 4.8 %collective-permute-done.20.refs_0_ = bf16[256,256]{1,0:T(8,128)(2,1)S(1)} collective-permute-done((bf16[256,256]{1,0:T(8,128)(2,1)S(1)}, bf16[256,256]{1,0:T(8,128)(2,1)S(1)}, u32[]{:S(2)}, u32[]{:S(2)}) %collective-permute-start.20) | collective-permute-done | bytes 131104 | tf_op jit(solution)/shard_map/ppermute | solution.py:316
  59.1 1.0 %collective-permute-start.27 = (bf16[256,256]{1,0:T(8,128)(2,1)S(1)}, bf16[256,256]{1,0:T(8,128)(2,1)S(1)}, u32[]{:S(2)}, u32[]{:S(2)}) collective-permute-start(bf16[256,256]{1,0:T(8,128)(2,1)S(1)} %total.1.after.refs_1_), channel_id=1, source_target_pairs={{0,16},{8,24},{16,0},{24,8},{1,17},{9,25},{17,1},{25,9},{2,18},{10... | collective-permute-start | bytes 393224 | tf_op jit(solution)/shard_map/ppermute | solution.py:316
  60.1 1.7 %collective-permute-done.24.refs_3_ = bf16[1536,256]{1,0:T(8,128)(2,1)S(1)} collective-permute-done((bf16[1536,256]{1,0:T(8,128)(2,1)S(1)}, bf16[1536,256]{1,0:T(8,128)(2,1)S(1)}, u32[]{:S(2)}, u32[]{:S(2)}) %collective-permute-start.24) | collective-permute-done | bytes 786464 | tf_op jit(solution)/shard_map/ppermute | solution.py:316
  63.5 1.5 %collective-permute-done.27.refs_0_ = bf16[256,256]{1,0:T(8,128)(2,1)S(1)} collective-permute-done((bf16[256,256]{1,0:T(8,128)(2,1)S(1)}, bf16[256,256]{1,0:T(8,128)(2,1)S(1)}, u32[]{:S(2)}, u32[]{:S(2)}) %collective-permute-start.27) | collective-permute-done | bytes 131104 | tf_op jit(solution)/shard_map/ppermute | solution.py:316
  65.3 1.4 %place.1.refs_1_ = bf16[128,8192]{1,0:T(8,128)(2,1)} custom-call(bf16[128,4096]{1,0:T(8,128)(2,1)S(1)} %get-tuple-element.52.mine.refs_0_, bf16[128,4096]{1,0:T(8,128)(2,1)S(1)} %collective-permute-done.25.came), custom_call_target="tpu_custom_call" | custom-call | flops 30000001024 | tf_op jit(solution)/shard_map/place/pallas_call | solution.py:292
  (54 shorter events, 11.7 us)
Async XLA Ops:
  0.6 10.3 %copy-start = (s32[1,128]{1,0:T(1,128)S(1)}, s32[1,128]{1,0:T(1,128)}, u32[]{:S(2)}) copy-start(s32[1,128]{1,0:T(1,128)} %seg_row.1) | copy-start | bytes 1540
  2.0 20.5 %collective-permute-start.5 = (bf16[256,1536]{1,0:T(8,128)(2,1)S(1)}, bf16[256,1536]{1,0:T(8,128)(2,1)S(1)}, u32[]{:S(2)}, u32[]{:S(2)}) collective-permute-start(bf16[256,1536]{1,0:T(8,128)(2,1)S(1)} %get-tuple-element.37), channel_id=1, source_target_pairs={{0,16},{8,24},{16,0},{24,8},{1,17},{9,25},{17,1},{25,9},{2,18},{10... | collective-permute-start | bytes 2359304 | tf_op jit(solution)/shard_map/ppermute | solution.py:316
  5.0 6.4 %collective-permute-start.1 = (bf16[256,256]{1,0:T(8,128)(2,1)S(1)}, bf16[256,256]{1,0:T(8,128)(2,1)S(1)}, u32[]{:S(2)}, u32[]{:S(2)}) collective-permute-start(bf16[256,256]{1,0:T(8,128)(2,1)S(1)} %get-tuple-element.31), channel_id=1, source_target_pairs={{0,2},{1,3},{2,0},{3,1},{4,6},{5,7},{6,4},{7,5},{8,10},{9,11},{10,... | collective-permute-start | bytes 393224 | tf_op jit(solution)/shard_map/ppermute | solution.py:316
  6.6 12.6 %collective-permute-start = (bf16[256,256]{1,0:T(8,128)(2,1)S(1)}, bf16[256,256]{1,0:T(8,128)(2,1)S(1)}, u32[]{:S(2)}, u32[]{:S(2)}) collective-permute-start(bf16[256,256]{1,0:T(8,128)(2,1)S(1)} %get-tuple-element.31), channel_id=1, source_target_pairs={{0,4},{1,5},{2,6},{3,7},{4,0},{5,1},{6,2},{7,3},{8,12},{9,13},{10,... | collective-permute-start | bytes 393224 | tf_op jit(solution)/shard_map/ppermute | solution.py:316
  9.2 11.6 %collective-permute-start.7 = (bf16[256,256]{1,0:T(8,128)(2,1)S(1)}, bf16[256,256]{1,0:T(8,128)(2,1)S(1)}, u32[]{:S(2)}, u32[]{:S(2)}) collective-permute-start(bf16[256,256]{1,0:T(8,128)(2,1)S(1)} %get-tuple-element.31), channel_id=1, source_target_pairs={{0,6},{1,7},{2,4},{3,5},{4,2},{5,3},{6,0},{7,1},{8,14},{9,15},{10,... | collective-permute-start | bytes 393224 | tf_op jit(solution)/shard_map/ppermute | solution.py:316
  9.4 12.1 %collective-permute-start.3 = (bf16[512,256]{1,0:T(8,128)(2,1)S(1)}, bf16[512,256]{1,0:T(8,128)(2,1)S(1)}, u32[]{:S(2)}, u32[]{:S(2)}) collective-permute-start(bf16[512,256]{1,0:T(8,128)(2,1)S(1)} %get-tuple-element.32.refs_1_.refs_0_), channel_id=1, source_target_pairs={{0,1},{1,0},{2,3},{3,2},{4,5},{5,4},{6,7},{7,6},{8,9},{9,8},{10,11... | collective-permute-start | bytes 786440 | tf_op jit(solution)/shard_map/ppermute | solution.py:316
  11.5 10.0 %collective-permute-start.2 = (bf16[256,256]{1,0:T(8,128)(2,1)S(1)}, bf16[256,256]{1,0:T(8,128)(2,1)S(1)}, u32[]{:S(2)}, u32[]{:S(2)}) collective-permute-start(bf16[256,256]{1,0:T(8,128)(2,1)S(1)} %collective-permute-done.1.refs_3_.refs_0_), channel_id=1, source_target_pairs={{0,1},{1,0},{2,3},{3,2},{4,5},{5,4},{6,7},{7,6},{8,9},{9,8},{10,11... | collective-permute-start | bytes 393224 | tf_op jit(solution)/shard_map/ppermute | solution.py:316
  19.3 5.0 %collective-permute-start.6 = (bf16[256,256]{1,0:T(8,128)(2,1)S(1)}, bf16[256,256]{1,0:T(8,128)(2,1)S(1)}, u32[]{:S(2)}, u32[]{:S(2)}) collective-permute-start(bf16[256,256]{1,0:T(8,128)(2,1)S(1)} %collective-permute-done.refs_1_.refs_5_.refs_2_), channel_id=1, source_target_pairs={{0,1},{1,0},{2,3},{3,2},{4,5},{5,4},{6,7},{7,6},{8,9},{9,8},{10,11... | collective-permute-start | bytes 393224 | tf_op jit(solution)/shard_map/ppermute | solution.py:316
  20.8 5.0 %collective-permute-start.8 = (bf16[256,256]{1,0:T(8,128)(2,1)S(1)}, bf16[256,256]{1,0:T(8,128)(2,1)S(1)}, u32[]{:S(2)}, u32[]{:S(2)}) collective-permute-start(bf16[256,256]{1,0:T(8,128)(2,1)S(1)} %collective-permute-done.7.refs_7_.refs_4_), channel_id=1, source_target_pairs={{0,1},{1,0},{2,3},{3,2},{4,5},{5,4},{6,7},{7,6},{8,9},{9,8},{10,11... | collective-permute-start | bytes 393224 | tf_op jit(solution)/shard_map/ppermute | solution.py:316
  21.5 4.3 %collective-permute-start.4 = (bf16[128,2560]{1,0:T(8,128)(2,1)S(1)}, bf16[128,2560]{1,0:T(8,128)(2,1)S(1)}, u32[]{:S(2)}, u32[]{:S(2)}) collective-permute-start(bf16[128,2560]{1,0:T(8,128)(2,1)S(1)} %gate.8), channel_id=1, source_target_pairs={{0,8},{8,0},{16,24},{24,16},{1,9},{9,1},{17,25},{25,17},{2,10},{10... | collective-permute-start | bytes 1966088 | tf_op jit(solution)/shard_map/ppermute | solution.py:316
  22.6 4.4 %collective-permute-start.11 = (bf16[128,1536]{1,0:T(8,128)(2,1)S(1)}, bf16[128,1536]{1,0:T(8,128)(2,1)S(1)}, u32[]{:S(2)}, u32[]{:S(2)}) collective-permute-start(bf16[128,1536]{1,0:T(8,128)(2,1)S(1)} %hand_on.1), channel_id=1, source_target_pairs={{0,8},{8,0},{16,24},{24,16},{1,9},{9,1},{17,25},{25,17},{2,10},{10... | collective-permute-start | bytes 1179656 | tf_op jit(solution)/shard_map/ppermute | solution.py:316
  26.4 2.3 %collective-permute-start.9 = (bf16[128,256]{1,0:T(8,128)(2,1)S(1)}, bf16[128,256]{1,0:T(8,128)(2,1)S(1)}, u32[]{:S(2)}, u32[]{:S(2)}) collective-permute-start(bf16[128,256]{1,0:T(8,128)(2,1)S(1)} %get-tuple-element.39), channel_id=1, source_target_pairs={{0,8},{8,0},{16,24},{24,16},{1,9},{9,1},{17,25},{25,17},{2,10},{10... | collective-permute-start | bytes 196616 | tf_op jit(solution)/shard_map/ppermute | solution.py:316
  26.4 5.0 %collective-permute-start.10 = (bf16[128,256]{1,0:T(8,128)(2,1)S(1)}, bf16[128,256]{1,0:T(8,128)(2,1)S(1)}, u32[]{:S(2)}, u32[]{:S(2)}) collective-permute-start(bf16[128,256]{1,0:T(8,128)(2,1)S(1)} %get-tuple-element.40), channel_id=1, source_target_pairs={{0,16},{8,24},{16,0},{24,8},{1,17},{9,25},{17,1},{25,9},{2,18},{10... | collective-permute-start | bytes 196616 | tf_op jit(solution)/shard_map/ppermute | solution.py:316
  27.3 4.6 %collective-permute-start.12 = (bf16[128,256]{1,0:T(8,128)(2,1)S(1)}, bf16[128,256]{1,0:T(8,128)(2,1)S(1)}, u32[]{:S(2)}, u32[]{:S(2)}) collective-permute-start(bf16[128,256]{1,0:T(8,128)(2,1)S(1)} %project_last.1), channel_id=1, source_target_pairs={{0,24},{8,16},{16,8},{24,0},{1,25},{9,17},{17,9},{25,1},{2,26},{10... | collective-permute-start | bytes 196616 | tf_op jit(solution)/shard_map/ppermute | solution.py:316
  33.4 3.8 %collective-permute-start.15 = (bf16[128,256]{1,0:T(8,128)(2,1)S(1)}, bf16[128,256]{1,0:T(8,128)(2,1)S(1)}, u32[]{:S(2)}, u32[]{:S(2)}) collective-permute-start(bf16[128,256]{1,0:T(8,128)(2,1)S(1)} %get-tuple-element.41.refs_1_.refs_2_.grad), channel_id=1, source_target_pairs={{0,8},{8,0},{16,24},{24,16},{1,9},{9,1},{17,25},{25,17},{2,10},{10... | collective-permute-start | bytes 196616 | tf_op jit(solution)/shard_map/ppermute | solution.py:316
  33.6 4.6 %collective-permute-start.16 = (bf16[128,256]{1,0:T(8,128)(2,1)S(1)}, bf16[128,256]{1,0:T(8,128)(2,1)S(1)}, u32[]{:S(2)}, u32[]{:S(2)}) collective-permute-start(bf16[128,256]{1,0:T(8,128)(2,1)S(1)} %get-tuple-element.41.refs_1_.refs_2_.grad), channel_id=1, source_target_pairs={{0,16},{8,24},{16,0},{24,8},{1,17},{9,25},{17,1},{25,9},{2,18},{10... | collective-permute-start | bytes 196616 | tf_op jit(solution)/shard_map/ppermute | solution.py:316
  34.6 4.4 %collective-permute-start.17 = (bf16[128,256]{1,0:T(8,128)(2,1)S(1)}, bf16[128,256]{1,0:T(8,128)(2,1)S(1)}, u32[]{:S(2)}, u32[]{:S(2)}) collective-permute-start(bf16[128,256]{1,0:T(8,128)(2,1)S(1)} %get-tuple-element.41.refs_1_.refs_2_.grad), channel_id=1, source_target_pairs={{0,24},{8,16},{16,8},{24,0},{1,25},{9,17},{17,9},{25,1},{2,26},{10... | collective-permute-start | bytes 196616 | tf_op jit(solution)/shard_map/ppermute | solution.py:316
  35.2 7.6 %collective-permute-start.13 = (bf16[128,512]{1,0:T(8,128)(2,1)S(1)}, bf16[128,512]{1,0:T(8,128)(2,1)S(1)}, u32[]{:S(2)}, u32[]{:S(2)}) collective-permute-start(bf16[128,512]{1,0:T(8,128)(2,1)S(1)} %gate.9), channel_id=1, source_target_pairs={{0,16},{8,24},{16,0},{24,8},{1,17},{9,25},{17,1},{25,9},{2,18},{10... | collective-permute-start | bytes 393224 | tf_op jit(solution)/shard_map/ppermute | solution.py:316
  36.3 8.3 %collective-permute-start.14 = (bf16[128,512]{1,0:T(8,128)(2,1)S(1)}, bf16[128,512]{1,0:T(8,128)(2,1)S(1)}, u32[]{:S(2)}, u32[]{:S(2)}) collective-permute-start(bf16[128,512]{1,0:T(8,128)(2,1)S(1)} %gate.10), channel_id=1, source_target_pairs={{0,24},{8,16},{16,8},{24,0},{1,25},{9,17},{17,9},{25,1},{2,26},{10... | collective-permute-start | bytes 393224 | tf_op jit(solution)/shard_map/ppermute | solution.py:316
  39.6 6.4 %collective-permute-start.19 = (bf16[256,256]{1,0:T(8,128)(2,1)S(1)}, bf16[256,256]{1,0:T(8,128)(2,1)S(1)}, u32[]{:S(2)}, u32[]{:S(2)}) collective-permute-start(bf16[256,256]{1,0:T(8,128)(2,1)S(1)} %get-tuple-element.48), channel_id=1, source_target_pairs={{0,1},{1,0},{2,3},{3,2},{4,5},{5,4},{6,7},{7,6},{8,9},{9,8},{10,11... | collective-permute-start | bytes 393224 | tf_op jit(solution)/shard_map/ppermute | solution.py:316
  41.0 7.3 %collective-permute-start.21 = (bf16[256,256]{1,0:T(8,128)(2,1)S(1)}, bf16[256,256]{1,0:T(8,128)(2,1)S(1)}, u32[]{:S(2)}, u32[]{:S(2)}) collective-permute-start(bf16[256,256]{1,0:T(8,128)(2,1)S(1)} %get-tuple-element.50), channel_id=1, source_target_pairs={{0,1},{1,0},{2,3},{3,2},{4,5},{5,4},{6,7},{7,6},{8,9},{9,8},{10,11... | collective-permute-start | bytes 393224 | tf_op jit(solution)/shard_map/ppermute | solution.py:316
  41.7 20.1 %collective-permute-start.24 = (bf16[1536,256]{1,0:T(8,128)(2,1)S(1)}, bf16[1536,256]{1,0:T(8,128)(2,1)S(1)}, u32[]{:S(2)}, u32[]{:S(2)}) collective-permute-start(bf16[1536,256]{1,0:T(8,128)(2,1)S(1)} %gather.1.refs_2_), channel_id=1, source_target_pairs={{0,16},{8,24},{16,0},{24,8},{1,17},{9,25},{17,1},{25,9},{2,18},{10... | collective-permute-start | bytes 2359304 | tf_op jit(solution)/shard_map/ppermute | solution.py:316
  42.8 9.7 %collective-permute-start.18 = (bf16[512,256]{1,0:T(8,128)(2,1)S(1)}, bf16[512,256]{1,0:T(8,128)(2,1)S(1)}, u32[]{:S(2)}, u32[]{:S(2)}) collective-permute-start(bf16[512,256]{1,0:T(8,128)(2,1)S(1)} %gate.11), channel_id=1, source_target_pairs={{0,2},{1,3},{2,0},{3,1},{4,6},{5,7},{6,4},{7,5},{8,10},{9,11},{10,... | collective-permute-start | bytes 786440 | tf_op jit(solution)/shard_map/ppermute | solution.py:316
  46.0 13.0 %collective-permute-start.20 = (bf16[256,256]{1,0:T(8,128)(2,1)S(1)}, bf16[256,256]{1,0:T(8,128)(2,1)S(1)}, u32[]{:S(2)}, u32[]{:S(2)}) collective-permute-start(bf16[256,256]{1,0:T(8,128)(2,1)S(1)} %pair.2.refs_1_), channel_id=1, source_target_pairs={{0,4},{1,5},{2,6},{3,7},{4,0},{5,1},{6,2},{7,3},{8,12},{9,13},{10,... | collective-permute-start | bytes 393224 | tf_op jit(solution)/shard_map/ppermute | solution.py:316
  48.4 10.5 %collective-permute-start.22 = (bf16[256,256]{1,0:T(8,128)(2,1)S(1)}, bf16[256,256]{1,0:T(8,128)(2,1)S(1)}, u32[]{:S(2)}, u32[]{:S(2)}) collective-permute-start(bf16[256,256]{1,0:T(8,128)(2,1)S(1)} %pair.3.refs_1_), channel_id=1, source_target_pairs={{0,6},{1,7},{2,4},{3,5},{4,2},{5,3},{6,0},{7,1},{8,14},{9,15},{10,... | collective-permute-start | bytes 393224 | tf_op jit(solution)/shard_map/ppermute | solution.py:316
  52.6 6.3 %collective-permute-start.23 = (bf16[256,256]{1,0:T(8,128)(2,1)S(1)}, bf16[256,256]{1,0:T(8,128)(2,1)S(1)}, u32[]{:S(2)}, u32[]{:S(2)}) collective-permute-start(bf16[256,256]{1,0:T(8,128)(2,1)S(1)} %gate.14), channel_id=1, source_target_pairs={{0,1},{1,0},{2,3},{3,2},{4,5},{5,4},{6,7},{7,6},{8,9},{9,8},{10,11... | collective-permute-start | bytes 393224 | tf_op jit(solution)/shard_map/ppermute | solution.py:316
  59.0 3.6 %collective-permute-start.26 = (bf16[256,256]{1,0:T(8,128)(2,1)S(1)}, bf16[256,256]{1,0:T(8,128)(2,1)S(1)}, u32[]{:S(2)}, u32[]{:S(2)}) collective-permute-start(bf16[256,256]{1,0:T(8,128)(2,1)S(1)} %total.1.after.refs_1_), channel_id=1, source_target_pairs={{0,8},{8,0},{16,24},{24,16},{1,9},{9,1},{17,25},{25,17},{2,10},{10... | collective-permute-start | bytes 393224 | tf_op jit(solution)/shard_map/ppermute | solution.py:316
  59.1 5.9 %collective-permute-start.27 = (bf16[256,256]{1,0:T(8,128)(2,1)S(1)}, bf16[256,256]{1,0:T(8,128)(2,1)S(1)}, u32[]{:S(2)}, u32[]{:S(2)}) collective-permute-start(bf16[256,256]{1,0:T(8,128)(2,1)S(1)} %total.1.after.refs_1_), channel_id=1, source_target_pairs={{0,16},{8,24},{16,0},{24,8},{1,17},{9,25},{17,1},{25,9},{2,18},{10... | collective-permute-start | bytes 393224 | tf_op jit(solution)/shard_map/ppermute | solution.py:316
  62.5 2.7 %collective-permute-start.25 = (bf16[128,4096]{1,0:T(8,128)(2,1)S(1)}, bf16[128,4096]{1,0:T(8,128)(2,1)S(1)}, u32[]{:S(2)}, u32[]{:S(2)}) collective-permute-start(bf16[128,4096]{1,0:T(8,128)(2,1)S(1)} %get-tuple-element.53), channel_id=1, source_target_pairs={{0,8},{8,0},{16,24},{24,16},{1,9},{9,1},{17,25},{25,17},{2,10},{10... | collective-permute-start | bytes 3145736 | tf_op jit(solution)/shard_map/ppermute | solution.py:316
  65.0 1.7 %collective-permute-start.28 = (bf16[256,256]{1,0:T(8,128)(2,1)S(1)}, bf16[256,256]{1,0:T(8,128)(2,1)S(1)}, u32[]{:S(2)}, u32[]{:S(2)}) collective-permute-start(bf16[256,256]{1,0:T(8,128)(2,1)S(1)} %gate.15.refs_2_), channel_id=1, source_target_pairs={{0,8},{8,0},{16,24},{24,16},{1,9},{9,1},{17,25},{25,17},{2,10},{10... | collective-permute-start | bytes 393224 | tf_op jit(solution)/shard_map/ppermute | solution.py:316

commit v2 on v1

--- a/solution.py
+++ b/solution.py
@@ -173,7 +173,7 @@
 def weight_grad_kernel(plan, shards, own, partner, *refs):
     group, rows, part, half = plan.group, plan.rows, plan.part, plan.half
     others, refs = refs[: group - 2], refs[group - 2 :]
-    grads, outs = refs[:group], refs[group:]
+    grads, outs = refs[:group], refs[-1 - max(index for index, _ in shards.values()) :]
     r = lax.axis_index("rep")
     grad = jnp.concatenate([g[...] for g in grads], axis=0)
     inner = plan.sub(r) * part
@@ -381,33 +381,35 @@
         )
     terms = [terms[0]] + [swap(terms[d], "rep", d) for d in range(1, group)]
 
+    near_x = [swap(gate(a, corner), "rep", 2) for a in staged[5:6]]
     d_queries, d_keyval = call(
         functools.partial(attention_kernel, group), "attention",
-        [qs, dos, mask, *terms], [VMEM] * (3 + group),
+        [qs, dos, mask, *terms, *near_x], [VMEM] * (3 + group) + [ANY] * blocks,
         [shape(queries.shape, BF16), shape((rows, cols), BF16)], VMEM, loose=1, weight=FRONT,
     )
 
     grads = [d_keyval] + [swap(d_keyval, "rep", d) for d in range(1, group)]
     block = shape((part, cols), BF16)
+    mine = call(
+        functools.partial(gather_kernel, plan), "gather", [grads[1], *far], [ANY] + [VMEM] * plan.far,
+        [shape((plan.far * part, cols), BF16)], VMEM,
+    )
+    far_rows_all = [*mine, *cross(list(mine) * blocks)]
     places = {2: (0, 0), 3: (0, 1), **{e: (e - 3, 0) for e in range(4, shards)}}
     outs = [shape((2 * part, cols), BF16)] + [block] * (shards - 4)
     sums = list(call(
         functools.partial(weight_grad_kernel, plan, places), "weight_grad",
-        [own, partner, *far_x, *grads], [VMEM] * (2 * group), outs, VMEM,
+        [own, partner, *far_x, *grads], [VMEM] * (2 * group), outs, VMEM, weight=FRONT,
     ))
-    mine = call(
-        functools.partial(gather_kernel, plan), "gather", [sums[0], *far], [ANY] + [VMEM] * plan.far,
-        [shape((plan.far * part, cols), BF16)], VMEM,
-    )
-    far_rows_all = [*mine, *cross(list(mine) * blocks)]
-    near_x = [swap(gate(a, d_keyval), "rep", d + 2) for d, a in enumerate(staged[5:])]
+    near_x += [swap(gate(a, d_keyval), "rep", 3) for a in staged[6:]]
     held = []
 
-    beyond = swap(gate(sums[0], *near_x[:1]), "shard", 2)
+    beyond = swap(gate(sums[0], *near_x[1:]), "shard", 2)
 
     def pair(d):
-        came = swap(sums[places[2 * d + 1][0]], "shard", 1)
-        mine = gate(sums[places[2 * d][0]], *held[-1:], weight=FRONT)
+        term = sums[places[2 * d + 1][0]]
+        came = swap(gate(term, *near_x[1:]) if d > 2 else term, "shard", 1)
+        mine = gate(sums[places[2 * d][0]], *held[-1:], weight=SLIGHT // 2)
         out = call(pair_kernel, "pair", [mine, came], [VMEM] * 2, [block], VMEM)[0]
         held.append(out)
         return out
@@ -416,7 +418,7 @@
     total = [swap(pairs[d], "shard", 2 * d) for d in range(2, lines)]
     near_terms = call(
         functools.partial(weight_grad_kernel, plan, {0: (0, 0), 1: (1, 0)}), "weight_grad_near",
-        [own, partner, *near_x, *grads], [VMEM] * (2 * group), [block] * 2, VMEM,
+        [own, partner, *near_x, *grads, pairs[2]], [VMEM] * (2 * group) + [ANY], [block] * 2, VMEM,
     )
     keep, send = call(
         near_kernel, "near", [*near_terms, beyond], [VMEM] * 3, [shape((part, cols), F32), block], VMEM

time: 67.7 us -> 67.6 us (level)
  waiting for transfers between devices: 26.9 us -> 26 us
    ppermute x29, waiting for transfers between devices: 26.9 us -> 26 us  [swap(): return lax.ppermute(array, axis, [(i, i ^ flip) for i in range(size)])]
  transfers between devices with their start and end apart: 29 -> 29, of which waited for: 18 -> 16; matrix products, arithmetic and copies ran while one was open for 0% -> 0% of each run, Pallas kernels for 10% -> 10%
where the time goes in v2:
time: 67.6 us; the launch traced here: 67.3 us
  starting transfers between devices  29.8 us (44%)
  waiting for transfers between devices  26 us (38%)
  Pallas kernels  10.6 us (16%)
  between operations  0.81 us (1%)
    ppermute x29, starting transfers between devices, swap(): return lax.ppermute(array, axis, [(i, i ^ flip) for i in range(size)])  29.8 us
    ppermute x29, waiting for transfers between devices, swap(): return lax.ppermute(array, axis, [(i, i ^ flip) for i in range(size)])  26 us
    pallas_call x17, Pallas kernels, call(): pl.pallas_call(kernel, out_shape=tuple(shapes), in_specs=in_specs, out_sp...  10.5 us
  transfers between devices with their start and end apart: 29, of which 16 were waited for; matrix products, arithmetic and copies ran while one was open for 0% of the time, Pallas kernels for 10%

profile of v2, /device:TPU:0, one launch (start us, length us, event | category | flops | bytes accessed | tf_op | source)
XLA Modules:
  0.0 67.3 jit_solution(10115164903311187074)
XLA Ops:
  0.6 1.4 %cut.1 = (bf16[512,256]{1,0:T(8,128)(2,1)S(1)}, bf16[256,256]{1,0:T(8,128)(2,1)S(1)}, bf16[256,1536]{1,0:T(8,128)(2,1)S(1)}) custom-call(bf16[128,8192]{1,0:T(8,128)(2,1)} %x.3, bf16[1024,256]{1,0:T(8,128)(2,1)} %weight.1), custom_call_target="tpu_custom_call" | custom-call | tf_op jit(solution)/shard_map/cut/pallas_call | solution.py:292
  2.0 3.0 %collective-permute-start.6 = (bf16[256,1536]{1,0:T(8,128)(2,1)S(1)}, bf16[256,1536]{1,0:T(8,128)(2,1)S(1)}, u32[]{:S(2)}, u32[]{:S(2)}) collective-permute-start(bf16[256,1536]{1,0:T(8,128)(2,1)S(1)} %get-tuple-element.38), channel_id=1, source_target_pairs={{0,16},{8,24},{16,0},{24,8},{1,17},{9,25},{17,1},{25,9},{2,18},{10... | collective-permute-start | bytes 2359304 | tf_op jit(solution)/shard_map/ppermute | solution.py:316
  5.0 1.6 %collective-permute-start.1 = (bf16[256,256]{1,0:T(8,128)(2,1)S(1)}, bf16[256,256]{1,0:T(8,128)(2,1)S(1)}, u32[]{:S(2)}, u32[]{:S(2)}) collective-permute-start(bf16[256,256]{1,0:T(8,128)(2,1)S(1)} %get-tuple-element.31), channel_id=1, source_target_pairs={{0,2},{1,3},{2,0},{3,1},{4,6},{5,7},{6,4},{7,5},{8,10},{9,11},{10,... | collective-permute-start | bytes 393224 | tf_op jit(solution)/shard_map/ppermute | solution.py:316
  6.6 2.6 %collective-permute-start = (bf16[256,256]{1,0:T(8,128)(2,1)S(1)}, bf16[256,256]{1,0:T(8,128)(2,1)S(1)}, u32[]{:S(2)}, u32[]{:S(2)}) collective-permute-start(bf16[256,256]{1,0:T(8,128)(2,1)S(1)} %get-tuple-element.31), channel_id=1, source_target_pairs={{0,4},{1,5},{2,6},{3,7},{4,0},{5,1},{6,2},{7,3},{8,12},{9,13},{10,... | collective-permute-start | bytes 393224 | tf_op jit(solution)/shard_map/ppermute | solution.py:316
  9.4 1.5 %collective-permute-start.3 = (bf16[512,256]{1,0:T(8,128)(2,1)S(1)}, bf16[512,256]{1,0:T(8,128)(2,1)S(1)}, u32[]{:S(2)}, u32[]{:S(2)}) collective-permute-start(bf16[512,256]{1,0:T(8,128)(2,1)S(1)} %get-tuple-element.32.refs_1_.refs_0_), channel_id=1, source_target_pairs={{0,1},{1,0},{2,3},{3,2},{4,5},{5,4},{6,7},{7,6},{8,9},{9,8},{10,11... | collective-permute-start | bytes 786440 | tf_op jit(solution)/shard_map/ppermute | solution.py:316
  11.5 1.5 %collective-permute-start.2 = (bf16[256,256]{1,0:T(8,128)(2,1)S(1)}, bf16[256,256]{1,0:T(8,128)(2,1)S(1)}, u32[]{:S(2)}, u32[]{:S(2)}) collective-permute-start(bf16[256,256]{1,0:T(8,128)(2,1)S(1)} %collective-permute-done.1.refs_3_.refs_0_), channel_id=1, source_target_pairs={{0,1},{1,0},{2,3},{3,2},{4,5},{5,4},{6,7},{7,6},{8,9},{9,8},{10,11... | collective-permute-start | bytes 393224 | tf_op jit(solution)/shard_map/ppermute | solution.py:316
  13.0 1.7 %stage.1 = (bf16[128,2560]{1,0:T(8,128)(2,1)S(1)}, bf16[512,128]{1,0:T(8,128)(2,1)S(1)}, bf16[512,128]{1,0:T(8,128)(2,1)S(1)}, f32[128,128]{1,0:T(8,128)S(1)}, b...) custom-call(bf16[128,8192]{1,0:T(8,128)(2,1)} %x.3, bf16[128,512]{1,0:T(8,128)(2,1)} %q.1, ...), custom_call_target="tpu_custom_call" | custom-call | flops 5000000000 | tf_op jit(solution)/shard_map/stage/pallas_call | solution.py:292
  14.7 4.6 %collective-permute-done.refs_1_.refs_5_.refs_2_ = bf16[256,256]{1,0:T(8,128)(2,1)S(1)} collective-permute-done((bf16[256,256]{1,0:T(8,128)(2,1)S(1)}, bf16[256,256]{1,0:T(8,128)(2,1)S(1)}, u32[]{:S(2)}, u32[]{:S(2)}) %collective-permute-start) | collective-permute-done | bytes 131104 | tf_op jit(solution)/shard_map/ppermute | solution.py:316
  19.3 1.5 %collective-permute-start.7 = (bf16[256,256]{1,0:T(8,128)(2,1)S(1)}, bf16[256,256]{1,0:T(8,128)(2,1)S(1)}, u32[]{:S(2)}, u32[]{:S(2)}) collective-permute-start(bf16[256,256]{1,0:T(8,128)(2,1)S(1)} %collective-permute-done.refs_1_.refs_5_.refs_2_), channel_id=1, source_target_pairs={{0,1},{1,0},{2,3},{3,2},{4,5},{5,4},{6,7},{7,6},{8,9},{9,8},{10,11... | collective-permute-start | bytes 393224 | tf_op jit(solution)/shard_map/ppermute | solution.py:316
  22.7 1.5 %collective-permute-done.7.refs_6_.refs_3_ = bf16[256,256]{1,0:T(8,128)(2,1)S(1)} collective-permute-done((bf16[256,256]{1,0:T(8,128)(2,1)S(1)}, bf16[256,256]{1,0:T(8,128)(2,1)S(1)}, u32[]{:S(2)}, u32[]{:S(2)}) %collective-permute-start.7) | collective-permute-done | bytes 131104 | tf_op jit(solution)/shard_map/ppermute | solution.py:316
  24.2 1.5 %collective-permute-done.9.refs_8_.refs_5_ = bf16[256,256]{1,0:T(8,128)(2,1)S(1)} collective-permute-done((bf16[256,256]{1,0:T(8,128)(2,1)S(1)}, bf16[256,256]{1,0:T(8,128)(2,1)S(1)}, u32[]{:S(2)}, u32[]{:S(2)}) %collective-permute-start.9) | collective-permute-done | bytes 131104 | tf_op jit(solution)/shard_map/ppermute | solution.py:316
  27.3 1.3 %collective-permute-start.13 = (bf16[128,256]{1,0:T(8,128)(2,1)S(1)}, bf16[128,256]{1,0:T(8,128)(2,1)S(1)}, u32[]{:S(2)}, u32[]{:S(2)}) collective-permute-start(bf16[128,256]{1,0:T(8,128)(2,1)S(1)} %project_last.1), channel_id=1, source_target_pairs={{0,24},{8,16},{16,8},{24,0},{1,25},{9,17},{17,9},{25,1},{2,26},{10... | collective-permute-start | bytes 196616 | tf_op jit(solution)/shard_map/ppermute | solution.py:316
  28.7 2.7 %collective-permute-done.11.refs_2_ = bf16[128,256]{1,0:T(8,128)(2,1)S(1)} collective-permute-done((bf16[128,256]{1,0:T(8,128)(2,1)S(1)}, bf16[128,256]{1,0:T(8,128)(2,1)S(1)}, u32[]{:S(2)}, u32[]{:S(2)}) %collective-permute-start.11) | collective-permute-done | bytes 65568 | tf_op jit(solution)/shard_map/ppermute | solution.py:316
  31.9 1.4 %attention.1 = (bf16[128,512]{1,0:T(8,128)(2,1)}, bf16[128,256]{1,0:T(8,128)(2,1)S(1)}) custom-call(bf16[512,128]{1,0:T(8,128)(2,1)S(1)} %get-tuple-element.35.qs_ref, bf16[512,128]{1,0:T(8,128)(2,1)S(1)} %get-tuple-element.36.dos_ref, f32[128,128]{1,0:T(8,128)S(1)} %get-tuple-element.37.mask, f32[128,256]{1,0:T(8,128)S(1)} %get-tuple-element.39.after.refs_0_, ...), custom_call_target="tpu_custom_call" | custom-call | flops 30000001024 | tf_op jit(solution)/shard_map/attention/pallas_call | solution.py:292
  33.6 0.9 %collective-permute-start.16 = (bf16[128,256]{1,0:T(8,128)(2,1)S(1)}, bf16[128,256]{1,0:T(8,128)(2,1)S(1)}, u32[]{:S(2)}, u32[]{:S(2)}) collective-permute-start(bf16[128,256]{1,0:T(8,128)(2,1)S(1)} %get-tuple-element.42.refs_1_.refs_2_.grad), channel_id=1, source_target_pairs={{0,16},{8,24},{16,0},{24,8},{1,17},{9,25},{17,1},{25,9},{2,18},{10... | collective-permute-start | bytes 196616 | tf_op jit(solution)/shard_map/ppermute | solution.py:316
  35.2 1.1 %collective-permute-start.14 = (bf16[128,512]{1,0:T(8,128)(2,1)S(1)}, bf16[128,512]{1,0:T(8,128)(2,1)S(1)}, u32[]{:S(2)}, u32[]{:S(2)}) collective-permute-start(bf16[128,512]{1,0:T(8,128)(2,1)S(1)} %gate.11), channel_id=1, source_target_pairs={{0,24},{8,16},{16,8},{24,0},{1,25},{9,17},{17,9},{25,1},{2,26},{10... | collective-permute-start | bytes 393224 | tf_op jit(solution)/shard_map/ppermute | solution.py:316
  36.4 1.2 %collective-permute-start.24 = (bf16[1536,256]{1,0:T(8,128)(2,1)S(1)}, bf16[1536,256]{1,0:T(8,128)(2,1)S(1)}, u32[]{:S(2)}, u32[]{:S(2)}) collective-permute-start(bf16[1536,256]{1,0:T(8,128)(2,1)S(1)} %gather.1.refs_2_), channel_id=1, source_target_pairs={{0,16},{8,24},{16,0},{24,8},{1,17},{9,25},{17,1},{25,9},{2,18},{10... | collective-permute-start | bytes 2359304 | tf_op jit(solution)/shard_map/ppermute | solution.py:316
  39.6 1.5 %collective-permute-start.18 = (bf16[256,256]{1,0:T(8,128)(2,1)S(1)}, bf16[256,256]{1,0:T(8,128)(2,1)S(1)}, u32[]{:S(2)}, u32[]{:S(2)}) collective-permute-start(bf16[256,256]{1,0:T(8,128)(2,1)S(1)} %get-tuple-element.44), channel_id=1, source_target_pairs={{0,1},{1,0},{2,3},{3,2},{4,5},{5,4},{6,7},{7,6},{8,9},{9,8},{10,11... | collective-permute-start | bytes 393224 | tf_op jit(solution)/shard_map/ppermute | solution.py:316
  41.8 0.8 %collective-permute-start.19 = (bf16[512,256]{1,0:T(8,128)(2,1)S(1)}, bf16[512,256]{1,0:T(8,128)(2,1)S(1)}, u32[]{:S(2)}, u32[]{:S(2)}) collective-permute-start(bf16[512,256]{1,0:T(8,128)(2,1)S(1)} %gate.13), channel_id=1, source_target_pairs={{0,2},{1,3},{2,0},{3,1},{4,6},{5,7},{6,4},{7,5},{8,10},{9,11},{10,... | collective-permute-start | bytes 786440 | tf_op jit(solution)/shard_map/ppermute | solution.py:316
  42.6 1.6 %collective-permute-start.21 = (bf16[256,256]{1,0:T(8,128)(2,1)S(1)}, bf16[256,256]{1,0:T(8,128)(2,1)S(1)}, u32[]{:S(2)}, u32[]{:S(2)}) collective-permute-start(bf16[256,256]{1,0:T(8,128)(2,1)S(1)} %gate.15), channel_id=1, source_target_pairs={{0,1},{1,0},{2,3},{3,2},{4,5},{5,4},{6,7},{7,6},{8,9},{9,8},{10,11... | collective-permute-start | bytes 393224 | tf_op jit(solution)/shard_map/ppermute | solution.py:316
  44.2 1.8 %collective-permute-done.18.came = bf16[256,256]{1,0:T(8,128)(2,1)S(1)} collective-permute-done((bf16[256,256]{1,0:T(8,128)(2,1)S(1)}, bf16[256,256]{1,0:T(8,128)(2,1)S(1)}, u32[]{:S(2)}, u32[]{:S(2)}) %collective-permute-start.18) | collective-permute-done | bytes 131104 | tf_op jit(solution)/shard_map/ppermute | solution.py:316
  46.0 1.4 %collective-permute-start.20 = (bf16[256,256]{1,0:T(8,128)(2,1)S(1)}, bf16[256,256]{1,0:T(8,128)(2,1)S(1)}, u32[]{:S(2)}, u32[]{:S(2)}) collective-permute-start(bf16[256,256]{1,0:T(8,128)(2,1)S(1)} %pair.2.refs_6_.refs_1_), channel_id=1, source_target_pairs={{0,4},{1,5},{2,6},{3,7},{4,0},{5,1},{6,2},{7,3},{8,12},{9,13},{10,... | collective-permute-start | bytes 393224 | tf_op jit(solution)/shard_map/ppermute | solution.py:316
  47.8 0.9 %collective-permute-done.21.came = bf16[256,256]{1,0:T(8,128)(2,1)S(1)} collective-permute-done((bf16[256,256]{1,0:T(8,128)(2,1)S(1)}, bf16[256,256]{1,0:T(8,128)(2,1)S(1)}, u32[]{:S(2)}, u32[]{:S(2)}) %collective-permute-start.21) | collective-permute-done | bytes 131104 | tf_op jit(solution)/shard_map/ppermute | solution.py:316
  48.7 2.7 %collective-permute-start.22 = (bf16[256,256]{1,0:T(8,128)(2,1)S(1)}, bf16[256,256]{1,0:T(8,128)(2,1)S(1)}, u32[]{:S(2)}, u32[]{:S(2)}) collective-permute-start(bf16[256,256]{1,0:T(8,128)(2,1)S(1)} %pair.3.refs_1_), channel_id=1, source_target_pairs={{0,6},{1,7},{2,4},{3,5},{4,2},{5,3},{6,0},{7,1},{8,14},{9,15},{10,... | collective-permute-start | bytes 393224 | tf_op jit(solution)/shard_map/ppermute | solution.py:316
  51.4 1.0 %collective-permute-done.19.came = bf16[512,256]{1,0:T(8,128)(2,1)S(1)} collective-permute-done((bf16[512,256]{1,0:T(8,128)(2,1)S(1)}, bf16[512,256]{1,0:T(8,128)(2,1)S(1)}, u32[]{:S(2)}, u32[]{:S(2)}) %collective-permute-start.19) | collective-permute-done | bytes 262176 | tf_op jit(solution)/shard_map/ppermute | solution.py:316
  52.5 1.5 %collective-permute-start.23 = (bf16[256,256]{1,0:T(8,128)(2,1)S(1)}, bf16[256,256]{1,0:T(8,128)(2,1)S(1)}, u32[]{:S(2)}, u32[]{:S(2)}) collective-permute-start(bf16[256,256]{1,0:T(8,128)(2,1)S(1)} %gate.16), channel_id=1, source_target_pairs={{0,1},{1,0},{2,3},{3,2},{4,5},{5,4},{6,7},{7,6},{8,9},{9,8},{10,11... | collective-permute-start | bytes 393224 | tf_op jit(solution)/shard_map/ppermute | solution.py:316
  54.0 4.9 %collective-permute-done.20.refs_0_ = bf16[256,256]{1,0:T(8,128)(2,1)S(1)} collective-permute-done((bf16[256,256]{1,0:T(8,128)(2,1)S(1)}, bf16[256,256]{1,0:T(8,128)(2,1)S(1)}, u32[]{:S(2)}, u32[]{:S(2)}) %collective-permute-start.20) | collective-permute-done | bytes 131104 | tf_op jit(solution)/shard_map/ppermute | solution.py:316
  59.1 1.0 %collective-permute-start.27 = (bf16[256,256]{1,0:T(8,128)(2,1)S(1)}, bf16[256,256]{1,0:T(8,128)(2,1)S(1)}, u32[]{:S(2)}, u32[]{:S(2)}) collective-permute-start(bf16[256,256]{1,0:T(8,128)(2,1)S(1)} %total.1.after.refs_1_), channel_id=1, source_target_pairs={{0,16},{8,24},{16,0},{24,8},{1,17},{9,25},{17,1},{25,9},{2,18},{10... | collective-permute-start | bytes 393224 | tf_op jit(solution)/shard_map/ppermute | solution.py:316
  61.1 0.8 %rows.2.refs_1_.refs_0_ = f32[1024,256]{1,0:T(8,128)} custom-call(bf16[128,4096]{1,0:T(8,128)(2,1)S(1)} %get-tuple-element.52.mine.refs_0_, bf16[256,256]{1,0:T(8,128)(2,1)S(1)} %total.1.after.refs_1_, bf16[256,256]{1,0:T(8,128)(2,1)S(1)} %collective-permute-done.26.refs_2_), custom_call_target="tpu_custom_call" | custom-call | tf_op jit(solution)/shard_map/rows/pallas_call | solution.py:292
  61.9 3.1 %collective-permute-done.27.refs_0_ = bf16[256,256]{1,0:T(8,128)(2,1)S(1)} collective-permute-done((bf16[256,256]{1,0:T(8,128)(2,1)S(1)}, bf16[256,256]{1,0:T(8,128)(2,1)S(1)}, u32[]{:S(2)}, u32[]{:S(2)}) %collective-permute-start.27) | collective-permute-done | bytes 131104 | tf_op jit(solution)/shard_map/ppermute | solution.py:316
  65.0 1.5 %place.1.refs_1_ = bf16[128,8192]{1,0:T(8,128)(2,1)} custom-call(bf16[128,4096]{1,0:T(8,128)(2,1)S(1)} %get-tuple-element.52.mine.refs_0_, bf16[128,4096]{1,0:T(8,128)(2,1)S(1)} %collective-permute-done.25.came), custom_call_target="tpu_custom_call" | custom-call | flops 30000001024 | tf_op jit(solution)/shard_map/place/pallas_call | solution.py:292
  66.5 0.8 %rows.3 = f32[1024,256]{1,0:T(8,128)} custom-call(f32[1024,256]{1,0:T(8,128)} %rows.2.refs_1_.refs_0_, bf16[128,8192]{1,0:T(8,128)(2,1)} %place.1.refs_1_, bf16[256,256]{1,0:T(8,128)(2,1)S(1)} %gate.17.refs_2_, bf16[256,256]{1,0:T(8,128)(2,1)S(1)} %collective-permute-done.28.refs_3_), custom_call_target="tpu_custom_call", output_to_operand_aliasing={{}: (0, {})} | custom-call | tf_op jit(solution)/shard_map/rows/pallas_call | solution.py:292
  (55 shorter events, 10.1 us)
Async XLA Ops:
  0.6 10.3 %copy-start = (s32[1,128]{1,0:T(1,128)S(1)}, s32[1,128]{1,0:T(1,128)}, u32[]{:S(2)}) copy-start(s32[1,128]{1,0:T(1,128)} %seg_row.1) | copy-start | bytes 1540
  2.0 20.5 %collective-permute-start.6 = (bf16[256,1536]{1,0:T(8,128)(2,1)S(1)}, bf16[256,1536]{1,0:T(8,128)(2,1)S(1)}, u32[]{:S(2)}, u32[]{:S(2)}) collective-permute-start(bf16[256,1536]{1,0:T(8,128)(2,1)S(1)} %get-tuple-element.38), channel_id=1, source_target_pairs={{0,16},{8,24},{16,0},{24,8},{1,17},{9,25},{17,1},{25,9},{2,18},{10... | collective-permute-start | bytes 2359304 | tf_op jit(solution)/shard_map/ppermute | solution.py:316
  5.0 6.4 %collective-permute-start.1 = (bf16[256,256]{1,0:T(8,128)(2,1)S(1)}, bf16[256,256]{1,0:T(8,128)(2,1)S(1)}, u32[]{:S(2)}, u32[]{:S(2)}) collective-permute-start(bf16[256,256]{1,0:T(8,128)(2,1)S(1)} %get-tuple-element.31), channel_id=1, source_target_pairs={{0,2},{1,3},{2,0},{3,1},{4,6},{5,7},{6,4},{7,5},{8,10},{9,11},{10,... | collective-permute-start | bytes 393224 | tf_op jit(solution)/shard_map/ppermute | solution.py:316
  6.6 12.6 %collective-permute-start = (bf16[256,256]{1,0:T(8,128)(2,1)S(1)}, bf16[256,256]{1,0:T(8,128)(2,1)S(1)}, u32[]{:S(2)}, u32[]{:S(2)}) collective-permute-start(bf16[256,256]{1,0:T(8,128)(2,1)S(1)} %get-tuple-element.31), channel_id=1, source_target_pairs={{0,4},{1,5},{2,6},{3,7},{4,0},{5,1},{6,2},{7,3},{8,12},{9,13},{10,... | collective-permute-start | bytes 393224 | tf_op jit(solution)/shard_map/ppermute | solution.py:316
  9.2 11.6 %collective-permute-start.8 = (bf16[256,256]{1,0:T(8,128)(2,1)S(1)}, bf16[256,256]{1,0:T(8,128)(2,1)S(1)}, u32[]{:S(2)}, u32[]{:S(2)}) collective-permute-start(bf16[256,256]{1,0:T(8,128)(2,1)S(1)} %get-tuple-element.31), channel_id=1, source_target_pairs={{0,6},{1,7},{2,4},{3,5},{4,2},{5,3},{6,0},{7,1},{8,14},{9,15},{10,... | collective-permute-start | bytes 393224 | tf_op jit(solution)/shard_map/ppermute | solution.py:316
  9.4 12.1 %collective-permute-start.3 = (bf16[512,256]{1,0:T(8,128)(2,1)S(1)}, bf16[512,256]{1,0:T(8,128)(2,1)S(1)}, u32[]{:S(2)}, u32[]{:S(2)}) collective-permute-start(bf16[512,256]{1,0:T(8,128)(2,1)S(1)} %get-tuple-element.32.refs_1_.refs_0_), channel_id=1, source_target_pairs={{0,1},{1,0},{2,3},{3,2},{4,5},{5,4},{6,7},{7,6},{8,9},{9,8},{10,11... | collective-permute-start | bytes 786440 | tf_op jit(solution)/shard_map/ppermute | solution.py:316
  11.5 10.0 %collective-permute-start.2 = (bf16[256,256]{1,0:T(8,128)(2,1)S(1)}, bf16[256,256]{1,0:T(8,128)(2,1)S(1)}, u32[]{:S(2)}, u32[]{:S(2)}) collective-permute-start(bf16[256,256]{1,0:T(8,128)(2,1)S(1)} %collective-permute-done.1.refs_3_.refs_0_), channel_id=1, source_target_pairs={{0,1},{1,0},{2,3},{3,2},{4,5},{5,4},{6,7},{7,6},{8,9},{9,8},{10,11... | collective-permute-start | bytes 393224 | tf_op jit(solution)/shard_map/ppermute | solution.py:316
  19.3 5.0 %collective-permute-start.7 = (bf16[256,256]{1,0:T(8,128)(2,1)S(1)}, bf16[256,256]{1,0:T(8,128)(2,1)S(1)}, u32[]{:S(2)}, u32[]{:S(2)}) collective-permute-start(bf16[256,256]{1,0:T(8,128)(2,1)S(1)} %collective-permute-done.refs_1_.refs_5_.refs_2_), channel_id=1, source_target_pairs={{0,1},{1,0},{2,3},{3,2},{4,5},{5,4},{6,7},{7,6},{8,9},{9,8},{10,11... | collective-permute-start | bytes 393224 | tf_op jit(solution)/shard_map/ppermute | solution.py:316
  20.8 5.0 %collective-permute-start.9 = (bf16[256,256]{1,0:T(8,128)(2,1)S(1)}, bf16[256,256]{1,0:T(8,128)(2,1)S(1)}, u32[]{:S(2)}, u32[]{:S(2)}) collective-permute-start(bf16[256,256]{1,0:T(8,128)(2,1)S(1)} %collective-permute-done.8.refs_7_.refs_4_), channel_id=1, source_target_pairs={{0,1},{1,0},{2,3},{3,2},{4,5},{5,4},{6,7},{7,6},{8,9},{9,8},{10,11... | collective-permute-start | bytes 393224 | tf_op jit(solution)/shard_map/ppermute | solution.py:316
  21.5 4.3 %collective-permute-start.4 = (bf16[128,2560]{1,0:T(8,128)(2,1)S(1)}, bf16[128,2560]{1,0:T(8,128)(2,1)S(1)}, u32[]{:S(2)}, u32[]{:S(2)}) collective-permute-start(bf16[128,2560]{1,0:T(8,128)(2,1)S(1)} %gate.9), channel_id=1, source_target_pairs={{0,8},{8,0},{16,24},{24,16},{1,9},{9,1},{17,25},{25,17},{2,10},{10... | collective-permute-start | bytes 1966088 | tf_op jit(solution)/shard_map/ppermute | solution.py:316
  21.5 7.2 %collective-permute-start.5 = (bf16[128,512]{1,0:T(8,128)(2,1)S(1)}, bf16[128,512]{1,0:T(8,128)(2,1)S(1)}, u32[]{:S(2)}, u32[]{:S(2)}) collective-permute-start(bf16[128,512]{1,0:T(8,128)(2,1)S(1)} %gate.10), channel_id=1, source_target_pairs={{0,16},{8,24},{16,0},{24,8},{1,17},{9,25},{17,1},{25,9},{2,18},{10... | collective-permute-start | bytes 393224 | tf_op jit(solution)/shard_map/ppermute | solution.py:316
  22.6 4.5 %collective-permute-start.12 = (bf16[128,1536]{1,0:T(8,128)(2,1)S(1)}, bf16[128,1536]{1,0:T(8,128)(2,1)S(1)}, u32[]{:S(2)}, u32[]{:S(2)}) collective-permute-start(bf16[128,1536]{1,0:T(8,128)(2,1)S(1)} %hand_on.1), channel_id=1, source_target_pairs={{0,8},{8,0},{16,24},{24,16},{1,9},{9,1},{17,25},{25,17},{2,10},{10... | collective-permute-start | bytes 1179656 | tf_op jit(solution)/shard_map/ppermute | solution.py:316
  26.4 2.3 %collective-permute-start.10 = (bf16[128,256]{1,0:T(8,128)(2,1)S(1)}, bf16[128,256]{1,0:T(8,128)(2,1)S(1)}, u32[]{:S(2)}, u32[]{:S(2)}) collective-permute-start(bf16[128,256]{1,0:T(8,128)(2,1)S(1)} %get-tuple-element.40), channel_id=1, source_target_pairs={{0,8},{8,0},{16,24},{24,16},{1,9},{9,1},{17,25},{25,17},{2,10},{10... | collective-permute-start | bytes 196616 | tf_op jit(solution)/shard_map/ppermute | solution.py:316
  26.5 5.0 %collective-permute-start.11 = (bf16[128,256]{1,0:T(8,128)(2,1)S(1)}, bf16[128,256]{1,0:T(8,128)(2,1)S(1)}, u32[]{:S(2)}, u32[]{:S(2)}) collective-permute-start(bf16[128,256]{1,0:T(8,128)(2,1)S(1)} %get-tuple-element.41), channel_id=1, source_target_pairs={{0,16},{8,24},{16,0},{24,8},{1,17},{9,25},{17,1},{25,9},{2,18},{10... | collective-permute-start | bytes 196616 | tf_op jit(solution)/shard_map/ppermute | solution.py:316
  27.3 4.6 %collective-permute-start.13 = (bf16[128,256]{1,0:T(8,128)(2,1)S(1)}, bf16[128,256]{1,0:T(8,128)(2,1)S(1)}, u32[]{:S(2)}, u32[]{:S(2)}) collective-permute-start(bf16[128,256]{1,0:T(8,128)(2,1)S(1)} %project_last.1), channel_id=1, source_target_pairs={{0,24},{8,16},{16,8},{24,0},{1,25},{9,17},{17,9},{25,1},{2,26},{10... | collective-permute-start | bytes 196616 | tf_op jit(solution)/shard_map/ppermute | solution.py:316
  33.4 2.9 %collective-permute-start.15 = (bf16[128,256]{1,0:T(8,128)(2,1)S(1)}, bf16[128,256]{1,0:T(8,128)(2,1)S(1)}, u32[]{:S(2)}, u32[]{:S(2)}) collective-permute-start(bf16[128,256]{1,0:T(8,128)(2,1)S(1)} %get-tuple-element.42.refs_1_.refs_2_.grad), channel_id=1, source_target_pairs={{0,8},{8,0},{16,24},{24,16},{1,9},{9,1},{17,25},{25,17},{2,10},{10... | collective-permute-start | bytes 196616 | tf_op jit(solution)/shard_map/ppermute | solution.py:316
  33.6 4.6 %collective-permute-start.16 = (bf16[128,256]{1,0:T(8,128)(2,1)S(1)}, bf16[128,256]{1,0:T(8,128)(2,1)S(1)}, u32[]{:S(2)}, u32[]{:S(2)}) collective-permute-start(bf16[128,256]{1,0:T(8,128)(2,1)S(1)} %get-tuple-element.42.refs_1_.refs_2_.grad), channel_id=1, source_target_pairs={{0,16},{8,24},{16,0},{24,8},{1,17},{9,25},{17,1},{25,9},{2,18},{10... | collective-permute-start | bytes 196616 | tf_op jit(solution)/shard_map/ppermute | solution.py:316
  34.6 4.4 %collective-permute-start.17 = (bf16[128,256]{1,0:T(8,128)(2,1)S(1)}, bf16[128,256]{1,0:T(8,128)(2,1)S(1)}, u32[]{:S(2)}, u32[]{:S(2)}) collective-permute-start(bf16[128,256]{1,0:T(8,128)(2,1)S(1)} %get-tuple-element.42.refs_1_.refs_2_.grad), channel_id=1, source_target_pairs={{0,24},{8,16},{16,8},{24,0},{1,25},{9,17},{17,9},{25,1},{2,26},{10... | collective-permute-start | bytes 196616 | tf_op jit(solution)/shard_map/ppermute | solution.py:316
  35.2 6.5 %collective-permute-start.14 = (bf16[128,512]{1,0:T(8,128)(2,1)S(1)}, bf16[128,512]{1,0:T(8,128)(2,1)S(1)}, u32[]{:S(2)}, u32[]{:S(2)}) collective-permute-start(bf16[128,512]{1,0:T(8,128)(2,1)S(1)} %gate.11), channel_id=1, source_target_pairs={{0,24},{8,16},{16,8},{24,0},{1,25},{9,17},{17,9},{25,1},{2,26},{10... | collective-permute-start | bytes 393224 | tf_op jit(solution)/shard_map/ppermute | solution.py:316
  36.4 23.7 %collective-permute-start.24 = (bf16[1536,256]{1,0:T(8,128)(2,1)S(1)}, bf16[1536,256]{1,0:T(8,128)(2,1)S(1)}, u32[]{:S(2)}, u32[]{:S(2)}) collective-permute-start(bf16[1536,256]{1,0:T(8,128)(2,1)S(1)} %gather.1.refs_2_), channel_id=1, source_target_pairs={{0,16},{8,24},{16,0},{24,8},{1,17},{9,25},{17,1},{25,9},{2,18},{10... | collective-permute-start | bytes 2359304 | tf_op jit(solution)/shard_map/ppermute | solution.py:316
  39.6 6.4 %collective-permute-start.18 = (bf16[256,256]{1,0:T(8,128)(2,1)S(1)}, bf16[256,256]{1,0:T(8,128)(2,1)S(1)}, u32[]{:S(2)}, u32[]{:S(2)}) collective-permute-start(bf16[256,256]{1,0:T(8,128)(2,1)S(1)} %get-tuple-element.44), channel_id=1, source_target_pairs={{0,1},{1,0},{2,3},{3,2},{4,5},{5,4},{6,7},{7,6},{8,9},{9,8},{10,11... | collective-permute-start | bytes 393224 | tf_op jit(solution)/shard_map/ppermute | solution.py:316
  41.8 10.7 %collective-permute-start.19 = (bf16[512,256]{1,0:T(8,128)(2,1)S(1)}, bf16[512,256]{1,0:T(8,128)(2,1)S(1)}, u32[]{:S(2)}, u32[]{:S(2)}) collective-permute-start(bf16[512,256]{1,0:T(8,128)(2,1)S(1)} %gate.13), channel_id=1, source_target_pairs={{0,2},{1,3},{2,0},{3,1},{4,6},{5,7},{6,4},{7,5},{8,10},{9,11},{10,... | collective-permute-start | bytes 786440 | tf_op jit(solution)/shard_map/ppermute | solution.py:316
  42.6 6.1 %collective-permute-start.21 = (bf16[256,256]{1,0:T(8,128)(2,1)S(1)}, bf16[256,256]{1,0:T(8,128)(2,1)S(1)}, u32[]{:S(2)}, u32[]{:S(2)}) collective-permute-start(bf16[256,256]{1,0:T(8,128)(2,1)S(1)} %gate.15), channel_id=1, source_target_pairs={{0,1},{1,0},{2,3},{3,2},{4,5},{5,4},{6,7},{7,6},{8,9},{9,8},{10,11... | collective-permute-start | bytes 393224 | tf_op jit(solution)/shard_map/ppermute | solution.py:316
  46.0 12.9 %collective-permute-start.20 = (bf16[256,256]{1,0:T(8,128)(2,1)S(1)}, bf16[256,256]{1,0:T(8,128)(2,1)S(1)}, u32[]{:S(2)}, u32[]{:S(2)}) collective-permute-start(bf16[256,256]{1,0:T(8,128)(2,1)S(1)} %pair.2.refs_6_.refs_1_), channel_id=1, source_target_pairs={{0,4},{1,5},{2,6},{3,7},{4,0},{5,1},{6,2},{7,3},{8,12},{9,13},{10,... | collective-permute-start | bytes 393224 | tf_op jit(solution)/shard_map/ppermute | solution.py:316
  48.7 10.2 %collective-permute-start.22 = (bf16[256,256]{1,0:T(8,128)(2,1)S(1)}, bf16[256,256]{1,0:T(8,128)(2,1)S(1)}, u32[]{:S(2)}, u32[]{:S(2)}) collective-permute-start(bf16[256,256]{1,0:T(8,128)(2,1)S(1)} %pair.3.refs_1_), channel_id=1, source_target_pairs={{0,6},{1,7},{2,4},{3,5},{4,2},{5,3},{6,0},{7,1},{8,14},{9,15},{10,... | collective-permute-start | bytes 393224 | tf_op jit(solution)/shard_map/ppermute | solution.py:316
  52.5 6.4 %collective-permute-start.23 = (bf16[256,256]{1,0:T(8,128)(2,1)S(1)}, bf16[256,256]{1,0:T(8,128)(2,1)S(1)}, u32[]{:S(2)}, u32[]{:S(2)}) collective-permute-start(bf16[256,256]{1,0:T(8,128)(2,1)S(1)} %gate.16), channel_id=1, source_target_pairs={{0,1},{1,0},{2,3},{3,2},{4,5},{5,4},{6,7},{7,6},{8,9},{9,8},{10,11... | collective-permute-start | bytes 393224 | tf_op jit(solution)/shard_map/ppermute | solution.py:316
  59.0 2.0 %collective-permute-start.26 = (bf16[256,256]{1,0:T(8,128)(2,1)S(1)}, bf16[256,256]{1,0:T(8,128)(2,1)S(1)}, u32[]{:S(2)}, u32[]{:S(2)}) collective-permute-start(bf16[256,256]{1,0:T(8,128)(2,1)S(1)} %total.1.after.refs_1_), channel_id=1, source_target_pairs={{0,8},{8,0},{16,24},{24,16},{1,9},{9,1},{17,25},{25,17},{2,10},{10... | collective-permute-start | bytes 393224 | tf_op jit(solution)/shard_map/ppermute | solution.py:316
  59.1 5.9 %collective-permute-start.27 = (bf16[256,256]{1,0:T(8,128)(2,1)S(1)}, bf16[256,256]{1,0:T(8,128)(2,1)S(1)}, u32[]{:S(2)}, u32[]{:S(2)}) collective-permute-start(bf16[256,256]{1,0:T(8,128)(2,1)S(1)} %total.1.after.refs_1_), channel_id=1, source_target_pairs={{0,16},{8,24},{16,0},{24,8},{1,17},{9,25},{17,1},{25,9},{2,18},{10... | collective-permute-start | bytes 393224 | tf_op jit(solution)/shard_map/ppermute | solution.py:316
  60.8 4.2 %collective-permute-start.25 = (bf16[128,4096]{1,0:T(8,128)(2,1)S(1)}, bf16[128,4096]{1,0:T(8,128)(2,1)S(1)}, u32[]{:S(2)}, u32[]{:S(2)}) collective-permute-start(bf16[128,4096]{1,0:T(8,128)(2,1)S(1)} %get-tuple-element.53), channel_id=1, source_target_pairs={{0,8},{8,0},{16,24},{24,16},{1,9},{9,1},{17,25},{25,17},{2,10},{10... | collective-permute-start | bytes 3145736 | tf_op jit(solution)/shard_map/ppermute | solution.py:316
  65.0 1.5 %collective-permute-start.28 = (bf16[256,256]{1,0:T(8,128)(2,1)S(1)}, bf16[256,256]{1,0:T(8,128)(2,1)S(1)}, u32[]{:S(2)}, u32[]{:S(2)}) collective-permute-start(bf16[256,256]{1,0:T(8,128)(2,1)S(1)} %gate.17.refs_2_), channel_id=1, source_target_pairs={{0,8},{8,0},{16,24},{24,16},{1,9},{9,1},{17,25},{25,17},{2,10},{10... | collective-permute-start | bytes 393224 | tf_op jit(solution)/shard_map/ppermute | solution.py:316

commit v3 on v2

--- a/solution.py
+++ b/solution.py
@@ -395,21 +395,29 @@
         [shape((plan.far * part, cols), BF16)], VMEM,
     )
     far_rows_all = [*mine, *cross(list(mine) * blocks)]
-    places = {2: (0, 0), 3: (0, 1), **{e: (e - 3, 0) for e in range(4, shards)}}
-    outs = [shape((2 * part, cols), BF16)] + [block] * (shards - 4)
-    sums = list(call(
-        functools.partial(weight_grad_kernel, plan, places), "weight_grad",
-        [own, partner, *far_x, *grads], [VMEM] * (2 * group), outs, VMEM, weight=FRONT,
-    ))
+    sums = []
+    for places, outs in (
+        ({5: (0, 0), 4: (1, 0)}, [block] * 2),
+        (
+            {2: (0, 0), 3: (0, 1), **{e: (e - 5, 0) for e in range(6, shards)}},
+            [shape((2 * part, cols), BF16)] + [block] * (shards - 6),
+        ),
+    ):
+        sums += call(
+            functools.partial(weight_grad_kernel, plan, places), "weight_grad",
+            [own, partner, *far_x, *grads, *sums], [VMEM] * (2 * group) + [ANY] * len(sums), outs, VMEM,
+            weight=0 if sums else FRONT,
+        )
+    sums = {e: term for e, term in zip((5, 4, 2, *range(6, shards)), sums)}
     near_x += [swap(gate(a, d_keyval), "rep", 3) for a in staged[6:]]
     held = []
 
-    beyond = swap(gate(sums[0], *near_x[1:]), "shard", 2)
+    beyond = swap(gate(sums[2], *near_x[1:]), "shard", 2)
 
     def pair(d):
-        term = sums[places[2 * d + 1][0]]
+        term = sums[2 * d + 1]
         came = swap(gate(term, *near_x[1:]) if d > 2 else term, "shard", 1)
-        mine = gate(sums[places[2 * d][0]], *held[-1:], weight=SLIGHT // 2)
+        mine = gate(sums[2 * d], *held[-1:], weight=SLIGHT // 2)
         out = call(pair_kernel, "pair", [mine, came], [VMEM] * 2, [block], VMEM)[0]
         held.append(out)
         return out

time: 67.6 us -> 67.4 us (level)
    pallas_call x17 -> x18, Pallas kernels: 10.5 us -> 10.7 us  [call(): pl.pallas_call(kernel, out_shape=tuple(shapes), in_specs=in_specs, out_sp...]
  transfers between devices with their start and end apart: 29 -> 29, of which waited for: 16 -> 16; matrix products, arithmetic and copies ran while one was open for 0% -> 0% of each run, Pallas kernels for 10% -> 11%
where the time goes in v3:
time: 67.4 us; the launch traced here: 67 us
  starting transfers between devices  29.6 us (44%)
  waiting for transfers between devices  25.7 us (38%)
  Pallas kernels  10.8 us (16%)
  between operations  0.82 us (1%)
    ppermute x29, starting transfers between devices, swap(): return lax.ppermute(array, axis, [(i, i ^ flip) for i in range(size)])  29.6 us
    ppermute x29, waiting for transfers between devices, swap(): return lax.ppermute(array, axis, [(i, i ^ flip) for i in range(size)])  25.7 us
    pallas_call x18, Pallas kernels, call(): pl.pallas_call(kernel, out_shape=tuple(shapes), in_specs=in_specs, out_sp...  10.7 us
  transfers between devices with their start and end apart: 29, of which 16 were waited for; matrix products, arithmetic and copies ran while one was open for 0% of the time, Pallas kernels for 11%

profile of v3, /device:TPU:0, one launch (start us, length us, event | category | flops | bytes accessed | tf_op | source)
XLA Modules:
  0.0 67.0 jit_solution(2772071401151541322)
XLA Ops:
  0.6 1.4 %cut.1 = (bf16[512,256]{1,0:T(8,128)(2,1)S(1)}, bf16[256,256]{1,0:T(8,128)(2,1)S(1)}, bf16[256,1536]{1,0:T(8,128)(2,1)S(1)}) custom-call(bf16[128,8192]{1,0:T(8,128)(2,1)} %x.3, bf16[1024,256]{1,0:T(8,128)(2,1)} %weight.1), custom_call_target="tpu_custom_call" | custom-call | tf_op jit(solution)/shard_map/cut/pallas_call | solution.py:292
  2.0 3.0 %collective-permute-start.6 = (bf16[256,1536]{1,0:T(8,128)(2,1)S(1)}, bf16[256,1536]{1,0:T(8,128)(2,1)S(1)}, u32[]{:S(2)}, u32[]{:S(2)}) collective-permute-start(bf16[256,1536]{1,0:T(8,128)(2,1)S(1)} %get-tuple-element.38), channel_id=1, source_target_pairs={{0,16},{8,24},{16,0},{24,8},{1,17},{9,25},{17,1},{25,9},{2,18},{10... | collective-permute-start | bytes 2359304 | tf_op jit(solution)/shard_map/ppermute | solution.py:316
  5.0 1.6 %collective-permute-start.1 = (bf16[256,256]{1,0:T(8,128)(2,1)S(1)}, bf16[256,256]{1,0:T(8,128)(2,1)S(1)}, u32[]{:S(2)}, u32[]{:S(2)}) collective-permute-start(bf16[256,256]{1,0:T(8,128)(2,1)S(1)} %get-tuple-element.31), channel_id=1, source_target_pairs={{0,2},{1,3},{2,0},{3,1},{4,6},{5,7},{6,4},{7,5},{8,10},{9,11},{10,... | collective-permute-start | bytes 393224 | tf_op jit(solution)/shard_map/ppermute | solution.py:316
  6.6 2.6 %collective-permute-start = (bf16[256,256]{1,0:T(8,128)(2,1)S(1)}, bf16[256,256]{1,0:T(8,128)(2,1)S(1)}, u32[]{:S(2)}, u32[]{:S(2)}) collective-permute-start(bf16[256,256]{1,0:T(8,128)(2,1)S(1)} %get-tuple-element.31), channel_id=1, source_target_pairs={{0,4},{1,5},{2,6},{3,7},{4,0},{5,1},{6,2},{7,3},{8,12},{9,13},{10,... | collective-permute-start | bytes 393224 | tf_op jit(solution)/shard_map/ppermute | solution.py:316
  9.4 1.5 %collective-permute-start.3 = (bf16[512,256]{1,0:T(8,128)(2,1)S(1)}, bf16[512,256]{1,0:T(8,128)(2,1)S(1)}, u32[]{:S(2)}, u32[]{:S(2)}) collective-permute-start(bf16[512,256]{1,0:T(8,128)(2,1)S(1)} %get-tuple-element.32.refs_1_.refs_0_), channel_id=1, source_target_pairs={{0,1},{1,0},{2,3},{3,2},{4,5},{5,4},{6,7},{7,6},{8,9},{9,8},{10,11... | collective-permute-start | bytes 786440 | tf_op jit(solution)/shard_map/ppermute | solution.py:316
  11.5 1.5 %collective-permute-start.2 = (bf16[256,256]{1,0:T(8,128)(2,1)S(1)}, bf16[256,256]{1,0:T(8,128)(2,1)S(1)}, u32[]{:S(2)}, u32[]{:S(2)}) collective-permute-start(bf16[256,256]{1,0:T(8,128)(2,1)S(1)} %collective-permute-done.1.refs_3_.refs_0_), channel_id=1, source_target_pairs={{0,1},{1,0},{2,3},{3,2},{4,5},{5,4},{6,7},{7,6},{8,9},{9,8},{10,11... | collective-permute-start | bytes 393224 | tf_op jit(solution)/shard_map/ppermute | solution.py:316
  13.0 1.7 %stage.1 = (bf16[128,2560]{1,0:T(8,128)(2,1)S(1)}, bf16[512,128]{1,0:T(8,128)(2,1)S(1)}, bf16[512,128]{1,0:T(8,128)(2,1)S(1)}, f32[128,128]{1,0:T(8,128)S(1)}, b...) custom-call(bf16[128,8192]{1,0:T(8,128)(2,1)} %x.3, bf16[128,512]{1,0:T(8,128)(2,1)} %q.1, ...), custom_call_target="tpu_custom_call" | custom-call | flops 5000000000 | tf_op jit(solution)/shard_map/stage/pallas_call | solution.py:292
  14.7 4.6 %collective-permute-done.refs_1_.refs_5_.refs_2_ = bf16[256,256]{1,0:T(8,128)(2,1)S(1)} collective-permute-done((bf16[256,256]{1,0:T(8,128)(2,1)S(1)}, bf16[256,256]{1,0:T(8,128)(2,1)S(1)}, u32[]{:S(2)}, u32[]{:S(2)}) %collective-permute-start) | collective-permute-done | bytes 131104 | tf_op jit(solution)/shard_map/ppermute | solution.py:316
  19.3 1.5 %collective-permute-start.7 = (bf16[256,256]{1,0:T(8,128)(2,1)S(1)}, bf16[256,256]{1,0:T(8,128)(2,1)S(1)}, u32[]{:S(2)}, u32[]{:S(2)}) collective-permute-start(bf16[256,256]{1,0:T(8,128)(2,1)S(1)} %collective-permute-done.refs_1_.refs_5_.refs_2_), channel_id=1, source_target_pairs={{0,1},{1,0},{2,3},{3,2},{4,5},{5,4},{6,7},{7,6},{8,9},{9,8},{10,11... | collective-permute-start | bytes 393224 | tf_op jit(solution)/shard_map/ppermute | solution.py:316
  22.7 1.5 %collective-permute-done.7.refs_6_.refs_3_ = bf16[256,256]{1,0:T(8,128)(2,1)S(1)} collective-permute-done((bf16[256,256]{1,0:T(8,128)(2,1)S(1)}, bf16[256,256]{1,0:T(8,128)(2,1)S(1)}, u32[]{:S(2)}, u32[]{:S(2)}) %collective-permute-start.7) | collective-permute-done | bytes 131104 | tf_op jit(solution)/shard_map/ppermute | solution.py:316
  24.2 1.5 %collective-permute-done.9.refs_8_.refs_5_ = bf16[256,256]{1,0:T(8,128)(2,1)S(1)} collective-permute-done((bf16[256,256]{1,0:T(8,128)(2,1)S(1)}, bf16[256,256]{1,0:T(8,128)(2,1)S(1)}, u32[]{:S(2)}, u32[]{:S(2)}) %collective-permute-start.9) | collective-permute-done | bytes 131104 | tf_op jit(solution)/shard_map/ppermute | solution.py:316
  27.3 1.3 %collective-permute-start.13 = (bf16[128,256]{1,0:T(8,128)(2,1)S(1)}, bf16[128,256]{1,0:T(8,128)(2,1)S(1)}, u32[]{:S(2)}, u32[]{:S(2)}) collective-permute-start(bf16[128,256]{1,0:T(8,128)(2,1)S(1)} %project_last.1), channel_id=1, source_target_pairs={{0,24},{8,16},{16,8},{24,0},{1,25},{9,17},{17,9},{25,1},{2,26},{10... | collective-permute-start | bytes 196616 | tf_op jit(solution)/shard_map/ppermute | solution.py:316
  28.7 2.7 %collective-permute-done.11.refs_2_ = bf16[128,256]{1,0:T(8,128)(2,1)S(1)} collective-permute-done((bf16[128,256]{1,0:T(8,128)(2,1)S(1)}, bf16[128,256]{1,0:T(8,128)(2,1)S(1)}, u32[]{:S(2)}, u32[]{:S(2)}) %collective-permute-start.11) | collective-permute-done | bytes 65568 | tf_op jit(solution)/shard_map/ppermute | solution.py:316
  31.9 1.4 %attention.1 = (bf16[128,512]{1,0:T(8,128)(2,1)}, bf16[128,256]{1,0:T(8,128)(2,1)S(1)}) custom-call(bf16[512,128]{1,0:T(8,128)(2,1)S(1)} %get-tuple-element.35.qs_ref, bf16[512,128]{1,0:T(8,128)(2,1)S(1)} %get-tuple-element.36.dos_ref, f32[128,128]{1,0:T(8,128)S(1)} %get-tuple-element.37.mask, f32[128,256]{1,0:T(8,128)S(1)} %get-tuple-element.39.after.refs_0_, ...), custom_call_target="tpu_custom_call" | custom-call | flops 30000001024 | tf_op jit(solution)/shard_map/attention/pallas_call | solution.py:292
  33.6 0.9 %collective-permute-start.16 = (bf16[128,256]{1,0:T(8,128)(2,1)S(1)}, bf16[128,256]{1,0:T(8,128)(2,1)S(1)}, u32[]{:S(2)}, u32[]{:S(2)}) collective-permute-start(bf16[128,256]{1,0:T(8,128)(2,1)S(1)} %get-tuple-element.42.refs_1_.refs_2_.grad), channel_id=1, source_target_pairs={{0,16},{8,24},{16,0},{24,8},{1,17},{9,25},{17,1},{25,9},{2,18},{10... | collective-permute-start | bytes 196616 | tf_op jit(solution)/shard_map/ppermute | solution.py:316
  35.2 1.1 %collective-permute-start.14 = (bf16[128,512]{1,0:T(8,128)(2,1)S(1)}, bf16[128,512]{1,0:T(8,128)(2,1)S(1)}, u32[]{:S(2)}, u32[]{:S(2)}) collective-permute-start(bf16[128,512]{1,0:T(8,128)(2,1)S(1)} %gate.11), channel_id=1, source_target_pairs={{0,24},{8,16},{16,8},{24,0},{1,25},{9,17},{17,9},{25,1},{2,26},{10... | collective-permute-start | bytes 393224 | tf_op jit(solution)/shard_map/ppermute | solution.py:316
  36.4 1.2 %collective-permute-start.24 = (bf16[1536,256]{1,0:T(8,128)(2,1)S(1)}, bf16[1536,256]{1,0:T(8,128)(2,1)S(1)}, u32[]{:S(2)}, u32[]{:S(2)}) collective-permute-start(bf16[1536,256]{1,0:T(8,128)(2,1)S(1)} %gather.1.refs_2_), channel_id=1, source_target_pairs={{0,16},{8,24},{16,0},{24,8},{1,17},{9,25},{17,1},{25,9},{2,18},{10... | collective-permute-start | bytes 2359304 | tf_op jit(solution)/shard_map/ppermute | solution.py:316
  39.3 1.5 %collective-permute-start.18 = (bf16[256,256]{1,0:T(8,128)(2,1)S(1)}, bf16[256,256]{1,0:T(8,128)(2,1)S(1)}, u32[]{:S(2)}, u32[]{:S(2)}) collective-permute-start(bf16[256,256]{1,0:T(8,128)(2,1)S(1)} %get-tuple-element.44.refs_6_), channel_id=1, source_target_pairs={{0,1},{1,0},{2,3},{3,2},{4,5},{5,4},{6,7},{7,6},{8,9},{9,8},{10,11... | collective-permute-start | bytes 393224 | tf_op jit(solution)/shard_map/ppermute | solution.py:316
  41.8 0.9 %collective-permute-start.19 = (bf16[512,256]{1,0:T(8,128)(2,1)S(1)}, bf16[512,256]{1,0:T(8,128)(2,1)S(1)}, u32[]{:S(2)}, u32[]{:S(2)}) collective-permute-start(bf16[512,256]{1,0:T(8,128)(2,1)S(1)} %gate.13), channel_id=1, source_target_pairs={{0,2},{1,3},{2,0},{3,1},{4,6},{5,7},{6,4},{7,5},{8,10},{9,11},{10,... | collective-permute-start | bytes 786440 | tf_op jit(solution)/shard_map/ppermute | solution.py:316
  42.6 1.5 %collective-permute-start.21 = (bf16[256,256]{1,0:T(8,128)(2,1)S(1)}, bf16[256,256]{1,0:T(8,128)(2,1)S(1)}, u32[]{:S(2)}, u32[]{:S(2)}) collective-permute-start(bf16[256,256]{1,0:T(8,128)(2,1)S(1)} %gate.15), channel_id=1, source_target_pairs={{0,1},{1,0},{2,3},{3,2},{4,5},{5,4},{6,7},{7,6},{8,9},{9,8},{10,11... | collective-permute-start | bytes 393224 | tf_op jit(solution)/shard_map/ppermute | solution.py:316
  44.2 1.4 %collective-permute-done.18.came = bf16[256,256]{1,0:T(8,128)(2,1)S(1)} collective-permute-done((bf16[256,256]{1,0:T(8,128)(2,1)S(1)}, bf16[256,256]{1,0:T(8,128)(2,1)S(1)}, u32[]{:S(2)}, u32[]{:S(2)}) %collective-permute-start.18) | collective-permute-done | bytes 131104 | tf_op jit(solution)/shard_map/ppermute | solution.py:316
  45.7 1.5 %collective-permute-start.20 = (bf16[256,256]{1,0:T(8,128)(2,1)S(1)}, bf16[256,256]{1,0:T(8,128)(2,1)S(1)}, u32[]{:S(2)}, u32[]{:S(2)}) collective-permute-start(bf16[256,256]{1,0:T(8,128)(2,1)S(1)} %pair.2.refs_6_.refs_1_), channel_id=1, source_target_pairs={{0,4},{1,5},{2,6},{3,7},{4,0},{5,1},{6,2},{7,3},{8,12},{9,13},{10,... | collective-permute-start | bytes 393224 | tf_op jit(solution)/shard_map/ppermute | solution.py:316
  47.5 0.9 %collective-permute-done.21.came = bf16[256,256]{1,0:T(8,128)(2,1)S(1)} collective-permute-done((bf16[256,256]{1,0:T(8,128)(2,1)S(1)}, bf16[256,256]{1,0:T(8,128)(2,1)S(1)}, u32[]{:S(2)}, u32[]{:S(2)}) %collective-permute-start.21) | collective-permute-done | bytes 131104 | tf_op jit(solution)/shard_map/ppermute | solution.py:316
  48.4 2.7 %collective-permute-start.22 = (bf16[256,256]{1,0:T(8,128)(2,1)S(1)}, bf16[256,256]{1,0:T(8,128)(2,1)S(1)}, u32[]{:S(2)}, u32[]{:S(2)}) collective-permute-start(bf16[256,256]{1,0:T(8,128)(2,1)S(1)} %pair.3.refs_1_), channel_id=1, source_target_pairs={{0,6},{1,7},{2,4},{3,5},{4,2},{5,3},{6,0},{7,1},{8,14},{9,15},{10,... | collective-permute-start | bytes 393224 | tf_op jit(solution)/shard_map/ppermute | solution.py:316
  51.1 1.4 %collective-permute-done.19.came = bf16[512,256]{1,0:T(8,128)(2,1)S(1)} collective-permute-done((bf16[512,256]{1,0:T(8,128)(2,1)S(1)}, bf16[512,256]{1,0:T(8,128)(2,1)S(1)}, u32[]{:S(2)}, u32[]{:S(2)}) %collective-permute-start.19) | collective-permute-done | bytes 262176 | tf_op jit(solution)/shard_map/ppermute | solution.py:316
  52.7 1.6 %collective-permute-start.23 = (bf16[256,256]{1,0:T(8,128)(2,1)S(1)}, bf16[256,256]{1,0:T(8,128)(2,1)S(1)}, u32[]{:S(2)}, u32[]{:S(2)}) collective-permute-start(bf16[256,256]{1,0:T(8,128)(2,1)S(1)} %gate.16), channel_id=1, source_target_pairs={{0,1},{1,0},{2,3},{3,2},{4,5},{5,4},{6,7},{7,6},{8,9},{9,8},{10,11... | collective-permute-start | bytes 393224 | tf_op jit(solution)/shard_map/ppermute | solution.py:316
  54.2 4.3 %collective-permute-done.20.refs_0_ = bf16[256,256]{1,0:T(8,128)(2,1)S(1)} collective-permute-done((bf16[256,256]{1,0:T(8,128)(2,1)S(1)}, bf16[256,256]{1,0:T(8,128)(2,1)S(1)}, u32[]{:S(2)}, u32[]{:S(2)}) %collective-permute-start.20) | collective-permute-done | bytes 131104 | tf_op jit(solution)/shard_map/ppermute | solution.py:316
  59.3 0.7 %input_grad.1 = (bf16[128,4096]{1,0:T(8,128)(2,1)S(1)}, bf16[128,4096]{1,0:T(8,128)(2,1)S(1)}) custom-call(bf16[256,256]{1,0:T(8,128)(2,1)S(1)} %total.1.after.refs_1_, bf16[128,256]{1,0:T(8,128)(2,1)S(1)} %get-tuple-element.42.refs_1_.refs_2_.grad, bf16[128,256]{1,0:T(8,128)(2,1)S(1)} %collective-permute-done.15.refs_3_.after.other, ...), custom_call_target="tpu_custom_call" | custom-call | tf_op jit(solution)/shard_map/input_grad/pallas_call | solution.py:292
  60.2 0.8 %rows.2.refs_1_.refs_0_ = f32[1024,256]{1,0:T(8,128)} custom-call(bf16[128,4096]{1,0:T(8,128)(2,1)S(1)} %get-tuple-element.52.mine.refs_0_, bf16[256,256]{1,0:T(8,128)(2,1)S(1)} %total.1.after.refs_1_, bf16[256,256]{1,0:T(8,128)(2,1)S(1)} %collective-permute-done.26.refs_2_), custom_call_target="tpu_custom_call" | custom-call | tf_op jit(solution)/shard_map/rows/pallas_call | solution.py:292
  61.1 3.5 %collective-permute-done.27.refs_0_ = bf16[256,256]{1,0:T(8,128)(2,1)S(1)} collective-permute-done((bf16[256,256]{1,0:T(8,128)(2,1)S(1)}, bf16[256,256]{1,0:T(8,128)(2,1)S(1)}, u32[]{:S(2)}, u32[]{:S(2)}) %collective-permute-start.27) | collective-permute-done | bytes 131104 | tf_op jit(solution)/shard_map/ppermute | solution.py:316
  64.6 1.5 %place.1.refs_1_ = bf16[128,8192]{1,0:T(8,128)(2,1)} custom-call(bf16[128,4096]{1,0:T(8,128)(2,1)S(1)} %get-tuple-element.52.mine.refs_0_, bf16[128,4096]{1,0:T(8,128)(2,1)S(1)} %collective-permute-done.25.came), custom_call_target="tpu_custom_call" | custom-call | flops 30000001024 | tf_op jit(solution)/shard_map/place/pallas_call | solution.py:292
  66.1 0.8 %rows.3 = f32[1024,256]{1,0:T(8,128)} custom-call(f32[1024,256]{1,0:T(8,128)} %rows.2.refs_1_.refs_0_, bf16[128,8192]{1,0:T(8,128)(2,1)} %place.1.refs_1_, bf16[256,256]{1,0:T(8,128)(2,1)S(1)} %gate.17.refs_2_, bf16[256,256]{1,0:T(8,128)(2,1)S(1)} %collective-permute-done.28.refs_3_), custom_call_target="tpu_custom_call", output_to_operand_aliasing={{}: (0, {})} | custom-call | tf_op jit(solution)/shard_map/rows/pallas_call | solution.py:292
  (56 shorter events, 9.8 us)
Async XLA Ops:
  0.6 10.3 %copy-start = (s32[1,128]{1,0:T(1,128)S(1)}, s32[1,128]{1,0:T(1,128)}, u32[]{:S(2)}) copy-start(s32[1,128]{1,0:T(1,128)} %seg_row.1) | copy-start | bytes 1540
  2.0 20.5 %collective-permute-start.6 = (bf16[256,1536]{1,0:T(8,128)(2,1)S(1)}, bf16[256,1536]{1,0:T(8,128)(2,1)S(1)}, u32[]{:S(2)}, u32[]{:S(2)}) collective-permute-start(bf16[256,1536]{1,0:T(8,128)(2,1)S(1)} %get-tuple-element.38), channel_id=1, source_target_pairs={{0,16},{8,24},{16,0},{24,8},{1,17},{9,25},{17,1},{25,9},{2,18},{10... | collective-permute-start | bytes 2359304 | tf_op jit(solution)/shard_map/ppermute | solution.py:316
  5.0 6.4 %collective-permute-start.1 = (bf16[256,256]{1,0:T(8,128)(2,1)S(1)}, bf16[256,256]{1,0:T(8,128)(2,1)S(1)}, u32[]{:S(2)}, u32[]{:S(2)}) collective-permute-start(bf16[256,256]{1,0:T(8,128)(2,1)S(1)} %get-tuple-element.31), channel_id=1, source_target_pairs={{0,2},{1,3},{2,0},{3,1},{4,6},{5,7},{6,4},{7,5},{8,10},{9,11},{10,... | collective-permute-start | bytes 393224 | tf_op jit(solution)/shard_map/ppermute | solution.py:316
  6.6 12.6 %collective-permute-start = (bf16[256,256]{1,0:T(8,128)(2,1)S(1)}, bf16[256,256]{1,0:T(8,128)(2,1)S(1)}, u32[]{:S(2)}, u32[]{:S(2)}) collective-permute-start(bf16[256,256]{1,0:T(8,128)(2,1)S(1)} %get-tuple-element.31), channel_id=1, source_target_pairs={{0,4},{1,5},{2,6},{3,7},{4,0},{5,1},{6,2},{7,3},{8,12},{9,13},{10,... | collective-permute-start | bytes 393224 | tf_op jit(solution)/shard_map/ppermute | solution.py:316
  9.2 11.6 %collective-permute-start.8 = (bf16[256,256]{1,0:T(8,128)(2,1)S(1)}, bf16[256,256]{1,0:T(8,128)(2,1)S(1)}, u32[]{:S(2)}, u32[]{:S(2)}) collective-permute-start(bf16[256,256]{1,0:T(8,128)(2,1)S(1)} %get-tuple-element.31), channel_id=1, source_target_pairs={{0,6},{1,7},{2,4},{3,5},{4,2},{5,3},{6,0},{7,1},{8,14},{9,15},{10,... | collective-permute-start | bytes 393224 | tf_op jit(solution)/shard_map/ppermute | solution.py:316
  9.4 12.1 %collective-permute-start.3 = (bf16[512,256]{1,0:T(8,128)(2,1)S(1)}, bf16[512,256]{1,0:T(8,128)(2,1)S(1)}, u32[]{:S(2)}, u32[]{:S(2)}) collective-permute-start(bf16[512,256]{1,0:T(8,128)(2,1)S(1)} %get-tuple-element.32.refs_1_.refs_0_), channel_id=1, source_target_pairs={{0,1},{1,0},{2,3},{3,2},{4,5},{5,4},{6,7},{7,6},{8,9},{9,8},{10,11... | collective-permute-start | bytes 786440 | tf_op jit(solution)/shard_map/ppermute | solution.py:316
  11.5 10.0 %collective-permute-start.2 = (bf16[256,256]{1,0:T(8,128)(2,1)S(1)}, bf16[256,256]{1,0:T(8,128)(2,1)S(1)}, u32[]{:S(2)}, u32[]{:S(2)}) collective-permute-start(bf16[256,256]{1,0:T(8,128)(2,1)S(1)} %collective-permute-done.1.refs_3_.refs_0_), channel_id=1, source_target_pairs={{0,1},{1,0},{2,3},{3,2},{4,5},{5,4},{6,7},{7,6},{8,9},{9,8},{10,11... | collective-permute-start | bytes 393224 | tf_op jit(solution)/shard_map/ppermute | solution.py:316
  19.3 5.0 %collective-permute-start.7 = (bf16[256,256]{1,0:T(8,128)(2,1)S(1)}, bf16[256,256]{1,0:T(8,128)(2,1)S(1)}, u32[]{:S(2)}, u32[]{:S(2)}) collective-permute-start(bf16[256,256]{1,0:T(8,128)(2,1)S(1)} %collective-permute-done.refs_1_.refs_5_.refs_2_), channel_id=1, source_target_pairs={{0,1},{1,0},{2,3},{3,2},{4,5},{5,4},{6,7},{7,6},{8,9},{9,8},{10,11... | collective-permute-start | bytes 393224 | tf_op jit(solution)/shard_map/ppermute | solution.py:316
  20.8 5.0 %collective-permute-start.9 = (bf16[256,256]{1,0:T(8,128)(2,1)S(1)}, bf16[256,256]{1,0:T(8,128)(2,1)S(1)}, u32[]{:S(2)}, u32[]{:S(2)}) collective-permute-start(bf16[256,256]{1,0:T(8,128)(2,1)S(1)} %collective-permute-done.8.refs_7_.refs_4_), channel_id=1, source_target_pairs={{0,1},{1,0},{2,3},{3,2},{4,5},{5,4},{6,7},{7,6},{8,9},{9,8},{10,11... | collective-permute-start | bytes 393224 | tf_op jit(solution)/shard_map/ppermute | solution.py:316
  21.5 4.3 %collective-permute-start.4 = (bf16[128,2560]{1,0:T(8,128)(2,1)S(1)}, bf16[128,2560]{1,0:T(8,128)(2,1)S(1)}, u32[]{:S(2)}, u32[]{:S(2)}) collective-permute-start(bf16[128,2560]{1,0:T(8,128)(2,1)S(1)} %gate.9), channel_id=1, source_target_pairs={{0,8},{8,0},{16,24},{24,16},{1,9},{9,1},{17,25},{25,17},{2,10},{10... | collective-permute-start | bytes 1966088 | tf_op jit(solution)/shard_map/ppermute | solution.py:316
  21.5 7.2 %collective-permute-start.5 = (bf16[128,512]{1,0:T(8,128)(2,1)S(1)}, bf16[128,512]{1,0:T(8,128)(2,1)S(1)}, u32[]{:S(2)}, u32[]{:S(2)}) collective-permute-start(bf16[128,512]{1,0:T(8,128)(2,1)S(1)} %gate.10), channel_id=1, source_target_pairs={{0,16},{8,24},{16,0},{24,8},{1,17},{9,25},{17,1},{25,9},{2,18},{10... | collective-permute-start | bytes 393224 | tf_op jit(solution)/shard_map/ppermute | solution.py:316
  22.6 4.4 %collective-permute-start.12 = (bf16[128,1536]{1,0:T(8,128)(2,1)S(1)}, bf16[128,1536]{1,0:T(8,128)(2,1)S(1)}, u32[]{:S(2)}, u32[]{:S(2)}) collective-permute-start(bf16[128,1536]{1,0:T(8,128)(2,1)S(1)} %hand_on.1), channel_id=1, source_target_pairs={{0,8},{8,0},{16,24},{24,16},{1,9},{9,1},{17,25},{25,17},{2,10},{10... | collective-permute-start | bytes 1179656 | tf_op jit(solution)/shard_map/ppermute | solution.py:316
  26.4 2.3 %collective-permute-start.10 = (bf16[128,256]{1,0:T(8,128)(2,1)S(1)}, bf16[128,256]{1,0:T(8,128)(2,1)S(1)}, u32[]{:S(2)}, u32[]{:S(2)}) collective-permute-start(bf16[128,256]{1,0:T(8,128)(2,1)S(1)} %get-tuple-element.40), channel_id=1, source_target_pairs={{0,8},{8,0},{16,24},{24,16},{1,9},{9,1},{17,25},{25,17},{2,10},{10... | collective-permute-start | bytes 196616 | tf_op jit(solution)/shard_map/ppermute | solution.py:316
  26.4 5.0 %collective-permute-start.11 = (bf16[128,256]{1,0:T(8,128)(2,1)S(1)}, bf16[128,256]{1,0:T(8,128)(2,1)S(1)}, u32[]{:S(2)}, u32[]{:S(2)}) collective-permute-start(bf16[128,256]{1,0:T(8,128)(2,1)S(1)} %get-tuple-element.41), channel_id=1, source_target_pairs={{0,16},{8,24},{16,0},{24,8},{1,17},{9,25},{17,1},{25,9},{2,18},{10... | collective-permute-start | bytes 196616 | tf_op jit(solution)/shard_map/ppermute | solution.py:316
  27.3 4.6 %collective-permute-start.13 = (bf16[128,256]{1,0:T(8,128)(2,1)S(1)}, bf16[128,256]{1,0:T(8,128)(2,1)S(1)}, u32[]{:S(2)}, u32[]{:S(2)}) collective-permute-start(bf16[128,256]{1,0:T(8,128)(2,1)S(1)} %project_last.1), channel_id=1, source_target_pairs={{0,24},{8,16},{16,8},{24,0},{1,25},{9,17},{17,9},{25,1},{2,26},{10... | collective-permute-start | bytes 196616 | tf_op jit(solution)/shard_map/ppermute | solution.py:316
  33.4 2.9 %collective-permute-start.15 = (bf16[128,256]{1,0:T(8,128)(2,1)S(1)}, bf16[128,256]{1,0:T(8,128)(2,1)S(1)}, u32[]{:S(2)}, u32[]{:S(2)}) collective-permute-start(bf16[128,256]{1,0:T(8,128)(2,1)S(1)} %get-tuple-element.42.refs_1_.refs_2_.grad), channel_id=1, source_target_pairs={{0,8},{8,0},{16,24},{24,16},{1,9},{9,1},{17,25},{25,17},{2,10},{10... | collective-permute-start | bytes 196616 | tf_op jit(solution)/shard_map/ppermute | solution.py:316
  33.6 4.6 %collective-permute-start.16 = (bf16[128,256]{1,0:T(8,128)(2,1)S(1)}, bf16[128,256]{1,0:T(8,128)(2,1)S(1)}, u32[]{:S(2)}, u32[]{:S(2)}) collective-permute-start(bf16[128,256]{1,0:T(8,128)(2,1)S(1)} %get-tuple-element.42.refs_1_.refs_2_.grad), channel_id=1, source_target_pairs={{0,16},{8,24},{16,0},{24,8},{1,17},{9,25},{17,1},{25,9},{2,18},{10... | collective-permute-start | bytes 196616 | tf_op jit(solution)/shard_map/ppermute | solution.py:316
  34.6 4.4 %collective-permute-start.17 = (bf16[128,256]{1,0:T(8,128)(2,1)S(1)}, bf16[128,256]{1,0:T(8,128)(2,1)S(1)}, u32[]{:S(2)}, u32[]{:S(2)}) collective-permute-start(bf16[128,256]{1,0:T(8,128)(2,1)S(1)} %get-tuple-element.42.refs_1_.refs_2_.grad), channel_id=1, source_target_pairs={{0,24},{8,16},{16,8},{24,0},{1,25},{9,17},{17,9},{25,1},{2,26},{10... | collective-permute-start | bytes 196616 | tf_op jit(solution)/shard_map/ppermute | solution.py:316
  35.2 6.5 %collective-permute-start.14 = (bf16[128,512]{1,0:T(8,128)(2,1)S(1)}, bf16[128,512]{1,0:T(8,128)(2,1)S(1)}, u32[]{:S(2)}, u32[]{:S(2)}) collective-permute-start(bf16[128,512]{1,0:T(8,128)(2,1)S(1)} %gate.11), channel_id=1, source_target_pairs={{0,24},{8,16},{16,8},{24,0},{1,25},{9,17},{17,9},{25,1},{2,26},{10... | collective-permute-start | bytes 393224 | tf_op jit(solution)/shard_map/ppermute | solution.py:316
  36.4 22.9 %collective-permute-start.24 = (bf16[1536,256]{1,0:T(8,128)(2,1)S(1)}, bf16[1536,256]{1,0:T(8,128)(2,1)S(1)}, u32[]{:S(2)}, u32[]{:S(2)}) collective-permute-start(bf16[1536,256]{1,0:T(8,128)(2,1)S(1)} %gather.1.refs_2_), channel_id=1, source_target_pairs={{0,16},{8,24},{16,0},{24,8},{1,17},{9,25},{17,1},{25,9},{2,18},{10... | collective-permute-start | bytes 2359304 | tf_op jit(solution)/shard_map/ppermute | solution.py:316
  39.3 6.3 %collective-permute-start.18 = (bf16[256,256]{1,0:T(8,128)(2,1)S(1)}, bf16[256,256]{1,0:T(8,128)(2,1)S(1)}, u32[]{:S(2)}, u32[]{:S(2)}) collective-permute-start(bf16[256,256]{1,0:T(8,128)(2,1)S(1)} %get-tuple-element.44.refs_6_), channel_id=1, source_target_pairs={{0,1},{1,0},{2,3},{3,2},{4,5},{5,4},{6,7},{7,6},{8,9},{9,8},{10,11... | collective-permute-start | bytes 393224 | tf_op jit(solution)/shard_map/ppermute | solution.py:316
  41.8 10.8 %collective-permute-start.19 = (bf16[512,256]{1,0:T(8,128)(2,1)S(1)}, bf16[512,256]{1,0:T(8,128)(2,1)S(1)}, u32[]{:S(2)}, u32[]{:S(2)}) collective-permute-start(bf16[512,256]{1,0:T(8,128)(2,1)S(1)} %gate.13), channel_id=1, source_target_pairs={{0,2},{1,3},{2,0},{3,1},{4,6},{5,7},{6,4},{7,5},{8,10},{9,11},{10,... | collective-permute-start | bytes 786440 | tf_op jit(solution)/shard_map/ppermute | solution.py:316
  42.6 5.8 %collective-permute-start.21 = (bf16[256,256]{1,0:T(8,128)(2,1)S(1)}, bf16[256,256]{1,0:T(8,128)(2,1)S(1)}, u32[]{:S(2)}, u32[]{:S(2)}) collective-permute-start(bf16[256,256]{1,0:T(8,128)(2,1)S(1)} %gate.15), channel_id=1, source_target_pairs={{0,1},{1,0},{2,3},{3,2},{4,5},{5,4},{6,7},{7,6},{8,9},{9,8},{10,11... | collective-permute-start | bytes 393224 | tf_op jit(solution)/shard_map/ppermute | solution.py:316
  45.7 12.9 %collective-permute-start.20 = (bf16[256,256]{1,0:T(8,128)(2,1)S(1)}, bf16[256,256]{1,0:T(8,128)(2,1)S(1)}, u32[]{:S(2)}, u32[]{:S(2)}) collective-permute-start(bf16[256,256]{1,0:T(8,128)(2,1)S(1)} %pair.2.refs_6_.refs_1_), channel_id=1, source_target_pairs={{0,4},{1,5},{2,6},{3,7},{4,0},{5,1},{6,2},{7,3},{8,12},{9,13},{10,... | collective-permute-start | bytes 393224 | tf_op jit(solution)/shard_map/ppermute | solution.py:316
  48.4 10.1 %collective-permute-start.22 = (bf16[256,256]{1,0:T(8,128)(2,1)S(1)}, bf16[256,256]{1,0:T(8,128)(2,1)S(1)}, u32[]{:S(2)}, u32[]{:S(2)}) collective-permute-start(bf16[256,256]{1,0:T(8,128)(2,1)S(1)} %pair.3.refs_1_), channel_id=1, source_target_pairs={{0,6},{1,7},{2,4},{3,5},{4,2},{5,3},{6,0},{7,1},{8,14},{9,15},{10,... | collective-permute-start | bytes 393224 | tf_op jit(solution)/shard_map/ppermute | solution.py:316
  52.7 5.9 %collective-permute-start.23 = (bf16[256,256]{1,0:T(8,128)(2,1)S(1)}, bf16[256,256]{1,0:T(8,128)(2,1)S(1)}, u32[]{:S(2)}, u32[]{:S(2)}) collective-permute-start(bf16[256,256]{1,0:T(8,128)(2,1)S(1)} %gate.16), channel_id=1, source_target_pairs={{0,1},{1,0},{2,3},{3,2},{4,5},{5,4},{6,7},{7,6},{8,9},{9,8},{10,11... | collective-permute-start | bytes 393224 | tf_op jit(solution)/shard_map/ppermute | solution.py:316
  58.6 1.6 %collective-permute-start.26 = (bf16[256,256]{1,0:T(8,128)(2,1)S(1)}, bf16[256,256]{1,0:T(8,128)(2,1)S(1)}, u32[]{:S(2)}, u32[]{:S(2)}) collective-permute-start(bf16[256,256]{1,0:T(8,128)(2,1)S(1)} %total.1.after.refs_1_), channel_id=1, source_target_pairs={{0,8},{8,0},{16,24},{24,16},{1,9},{9,1},{17,25},{25,17},{2,10},{10... | collective-permute-start | bytes 393224 | tf_op jit(solution)/shard_map/ppermute | solution.py:316
  58.7 5.9 %collective-permute-start.27 = (bf16[256,256]{1,0:T(8,128)(2,1)S(1)}, bf16[256,256]{1,0:T(8,128)(2,1)S(1)}, u32[]{:S(2)}, u32[]{:S(2)}) collective-permute-start(bf16[256,256]{1,0:T(8,128)(2,1)S(1)} %total.1.after.refs_1_), channel_id=1, source_target_pairs={{0,16},{8,24},{16,0},{24,8},{1,17},{9,25},{17,1},{25,9},{2,18},{10... | collective-permute-start | bytes 393224 | tf_op jit(solution)/shard_map/ppermute | solution.py:316
  60.0 4.6 %collective-permute-start.25 = (bf16[128,4096]{1,0:T(8,128)(2,1)S(1)}, bf16[128,4096]{1,0:T(8,128)(2,1)S(1)}, u32[]{:S(2)}, u32[]{:S(2)}) collective-permute-start(bf16[128,4096]{1,0:T(8,128)(2,1)S(1)} %get-tuple-element.53), channel_id=1, source_target_pairs={{0,8},{8,0},{16,24},{24,16},{1,9},{9,1},{17,25},{25,17},{2,10},{10... | collective-permute-start | bytes 3145736 | tf_op jit(solution)/shard_map/ppermute | solution.py:316
  64.6 1.5 %collective-permute-start.28 = (bf16[256,256]{1,0:T(8,128)(2,1)S(1)}, bf16[256,256]{1,0:T(8,128)(2,1)S(1)}, u32[]{:S(2)}, u32[]{:S(2)}) collective-permute-start(bf16[256,256]{1,0:T(8,128)(2,1)S(1)} %gate.17.refs_2_), channel_id=1, source_target_pairs={{0,8},{8,0},{16,24},{24,16},{1,9},{9,1},{17,25},{25,17},{2,10},{10... | collective-permute-start | bytes 393224 | tf_op jit(solution)/shard_map/ppermute | solution.py:316

commit v4 on v3

--- a/solution.py
+++ b/solution.py
@@ -107,7 +107,7 @@
     to = lax.broadcasted_iota(jnp.int32, (rows, rows), 0)
     of = lax.broadcasted_iota(jnp.int32, (rows, rows), 1)
     allowed = (seg_col[...] == seg_row[...]) & (of <= to)
-    mask[...] = allowed.astype(F32)
+    mask[...] = jnp.where(allowed, 0.0, -1e30)
     finish(copies)
 
 
@@ -150,13 +150,12 @@
         keyval += term[...].astype(F32)
     keys = keyval[:, :HEAD].astype(BF16)
     values = keyval[:, HEAD:].astype(BF16)
-    allowed = jnp.concatenate([mask[...]] * QH, axis=0) > 0.5
+    hidden = jnp.concatenate([mask[...]] * QH, axis=0)
     qs, dos = qs_ref[...], dos_ref[...]
-    scores = dot(qs, keys, ((1,), (1,))) * SCALE
+    scores = dot(qs, keys, ((1,), (1,))) * SCALE + hidden
     dprob = dot(dos, values, ((1,), (1,)))
-    scores = jnp.where(allowed, scores, -1e30)
     top = jnp.max(scores, axis=1, keepdims=True)
-    weights = jnp.where(allowed, jnp.exp(scores - top), 0.0)
+    weights = jnp.exp(scores - top)
     probs = weights / jnp.sum(weights, axis=1, keepdims=True)
     low = probs.astype(BF16)
     delta = jnp.sum(low.astype(F32) * dprob, axis=1, keepdims=True)

time: 67.4 us -> 67.4 us (level)
  no operation moved by 1% of the time
where the time goes in v4:
time: 67.4 us; the launch traced here: 67 us
  starting transfers between devices  29.6 us (44%)
  waiting for transfers between devices  25.7 us (38%)
  Pallas kernels  10.8 us (16%)
  between operations  0.82 us (1%)
    ppermute x29, starting transfers between devices, swap(): return lax.ppermute(array, axis, [(i, i ^ flip) for i in range(size)])  29.6 us
    ppermute x29, waiting for transfers between devices, swap(): return lax.ppermute(array, axis, [(i, i ^ flip) for i in range(size)])  25.7 us
    pallas_call x18, Pallas kernels, call(): pl.pallas_call(kernel, out_shape=tuple(shapes), in_specs=in_specs, out_sp...  10.8 us
  transfers between devices with their start and end apart: 29, of which 16 were waited for; matrix products, arithmetic and copies ran while one was open for 0% of the time, Pallas kernels for 11%

profile of v4, /device:TPU:0, one launch (start us, length us, event | category | flops | bytes accessed | tf_op | source)
XLA Modules:
  0.0 67.0 jit_solution(2112310063530464066)
XLA Ops:
  0.6 1.4 %cut.1 = (bf16[512,256]{1,0:T(8,128)(2,1)S(1)}, bf16[256,256]{1,0:T(8,128)(2,1)S(1)}, bf16[256,1536]{1,0:T(8,128)(2,1)S(1)}) custom-call(bf16[128,8192]{1,0:T(8,128)(2,1)} %x.3, bf16[1024,256]{1,0:T(8,128)(2,1)} %weight.1), custom_call_target="tpu_custom_call" | custom-call | tf_op jit(solution)/shard_map/cut/pallas_call | solution.py:291
  2.0 3.0 %collective-permute-start.6 = (bf16[256,1536]{1,0:T(8,128)(2,1)S(1)}, bf16[256,1536]{1,0:T(8,128)(2,1)S(1)}, u32[]{:S(2)}, u32[]{:S(2)}) collective-permute-start(bf16[256,1536]{1,0:T(8,128)(2,1)S(1)} %get-tuple-element.38), channel_id=1, source_target_pairs={{0,16},{8,24},{16,0},{24,8},{1,17},{9,25},{17,1},{25,9},{2,18},{10... | collective-permute-start | bytes 2359304 | tf_op jit(solution)/shard_map/ppermute | solution.py:315
  5.0 1.6 %collective-permute-start.1 = (bf16[256,256]{1,0:T(8,128)(2,1)S(1)}, bf16[256,256]{1,0:T(8,128)(2,1)S(1)}, u32[]{:S(2)}, u32[]{:S(2)}) collective-permute-start(bf16[256,256]{1,0:T(8,128)(2,1)S(1)} %get-tuple-element.31), channel_id=1, source_target_pairs={{0,2},{1,3},{2,0},{3,1},{4,6},{5,7},{6,4},{7,5},{8,10},{9,11},{10,... | collective-permute-start | bytes 393224 | tf_op jit(solution)/shard_map/ppermute | solution.py:315
  6.6 2.6 %collective-permute-start = (bf16[256,256]{1,0:T(8,128)(2,1)S(1)}, bf16[256,256]{1,0:T(8,128)(2,1)S(1)}, u32[]{:S(2)}, u32[]{:S(2)}) collective-permute-start(bf16[256,256]{1,0:T(8,128)(2,1)S(1)} %get-tuple-element.31), channel_id=1, source_target_pairs={{0,4},{1,5},{2,6},{3,7},{4,0},{5,1},{6,2},{7,3},{8,12},{9,13},{10,... | collective-permute-start | bytes 393224 | tf_op jit(solution)/shard_map/ppermute | solution.py:315
  9.4 1.5 %collective-permute-start.3 = (bf16[512,256]{1,0:T(8,128)(2,1)S(1)}, bf16[512,256]{1,0:T(8,128)(2,1)S(1)}, u32[]{:S(2)}, u32[]{:S(2)}) collective-permute-start(bf16[512,256]{1,0:T(8,128)(2,1)S(1)} %get-tuple-element.32.refs_1_.refs_0_), channel_id=1, source_target_pairs={{0,1},{1,0},{2,3},{3,2},{4,5},{5,4},{6,7},{7,6},{8,9},{9,8},{10,11... | collective-permute-start | bytes 786440 | tf_op jit(solution)/shard_map/ppermute | solution.py:315
  11.5 1.5 %collective-permute-start.2 = (bf16[256,256]{1,0:T(8,128)(2,1)S(1)}, bf16[256,256]{1,0:T(8,128)(2,1)S(1)}, u32[]{:S(2)}, u32[]{:S(2)}) collective-permute-start(bf16[256,256]{1,0:T(8,128)(2,1)S(1)} %collective-permute-done.1.refs_3_.refs_0_), channel_id=1, source_target_pairs={{0,1},{1,0},{2,3},{3,2},{4,5},{5,4},{6,7},{7,6},{8,9},{9,8},{10,11... | collective-permute-start | bytes 393224 | tf_op jit(solution)/shard_map/ppermute | solution.py:315
  13.0 1.7 %stage.1 = (bf16[128,2560]{1,0:T(8,128)(2,1)S(1)}, bf16[512,128]{1,0:T(8,128)(2,1)S(1)}, bf16[512,128]{1,0:T(8,128)(2,1)S(1)}, f32[128,128]{1,0:T(8,128)S(1)}, b...) custom-call(bf16[128,8192]{1,0:T(8,128)(2,1)} %x.3, bf16[128,512]{1,0:T(8,128)(2,1)} %q.1, ...), custom_call_target="tpu_custom_call" | custom-call | flops 5000000000 | tf_op jit(solution)/shard_map/stage/pallas_call | solution.py:291
  14.7 4.6 %collective-permute-done.refs_1_.refs_5_.refs_2_ = bf16[256,256]{1,0:T(8,128)(2,1)S(1)} collective-permute-done((bf16[256,256]{1,0:T(8,128)(2,1)S(1)}, bf16[256,256]{1,0:T(8,128)(2,1)S(1)}, u32[]{:S(2)}, u32[]{:S(2)}) %collective-permute-start) | collective-permute-done | bytes 131104 | tf_op jit(solution)/shard_map/ppermute | solution.py:315
  19.3 1.5 %collective-permute-start.7 = (bf16[256,256]{1,0:T(8,128)(2,1)S(1)}, bf16[256,256]{1,0:T(8,128)(2,1)S(1)}, u32[]{:S(2)}, u32[]{:S(2)}) collective-permute-start(bf16[256,256]{1,0:T(8,128)(2,1)S(1)} %collective-permute-done.refs_1_.refs_5_.refs_2_), channel_id=1, source_target_pairs={{0,1},{1,0},{2,3},{3,2},{4,5},{5,4},{6,7},{7,6},{8,9},{9,8},{10,11... | collective-permute-start | bytes 393224 | tf_op jit(solution)/shard_map/ppermute | solution.py:315
  22.7 1.5 %collective-permute-done.7.refs_6_.refs_3_ = bf16[256,256]{1,0:T(8,128)(2,1)S(1)} collective-permute-done((bf16[256,256]{1,0:T(8,128)(2,1)S(1)}, bf16[256,256]{1,0:T(8,128)(2,1)S(1)}, u32[]{:S(2)}, u32[]{:S(2)}) %collective-permute-start.7) | collective-permute-done | bytes 131104 | tf_op jit(solution)/shard_map/ppermute | solution.py:315
  24.2 1.5 %collective-permute-done.9.refs_8_.refs_5_ = bf16[256,256]{1,0:T(8,128)(2,1)S(1)} collective-permute-done((bf16[256,256]{1,0:T(8,128)(2,1)S(1)}, bf16[256,256]{1,0:T(8,128)(2,1)S(1)}, u32[]{:S(2)}, u32[]{:S(2)}) %collective-permute-start.9) | collective-permute-done | bytes 131104 | tf_op jit(solution)/shard_map/ppermute | solution.py:315
  27.3 1.3 %collective-permute-start.13 = (bf16[128,256]{1,0:T(8,128)(2,1)S(1)}, bf16[128,256]{1,0:T(8,128)(2,1)S(1)}, u32[]{:S(2)}, u32[]{:S(2)}) collective-permute-start(bf16[128,256]{1,0:T(8,128)(2,1)S(1)} %project_last.1), channel_id=1, source_target_pairs={{0,24},{8,16},{16,8},{24,0},{1,25},{9,17},{17,9},{25,1},{2,26},{10... | collective-permute-start | bytes 196616 | tf_op jit(solution)/shard_map/ppermute | solution.py:315
  28.7 2.7 %collective-permute-done.11.refs_2_ = bf16[128,256]{1,0:T(8,128)(2,1)S(1)} collective-permute-done((bf16[128,256]{1,0:T(8,128)(2,1)S(1)}, bf16[128,256]{1,0:T(8,128)(2,1)S(1)}, u32[]{:S(2)}, u32[]{:S(2)}) %collective-permute-start.11) | collective-permute-done | bytes 65568 | tf_op jit(solution)/shard_map/ppermute | solution.py:315
  31.9 1.4 %attention.1 = (bf16[128,512]{1,0:T(8,128)(2,1)}, bf16[128,256]{1,0:T(8,128)(2,1)S(1)}) custom-call(bf16[512,128]{1,0:T(8,128)(2,1)S(1)} %get-tuple-element.35.qs_ref, bf16[512,128]{1,0:T(8,128)(2,1)S(1)} %get-tuple-element.36.dos_ref, f32[128,128]{1,0:T(8,128)S(1)} %get-tuple-element.37.mask, f32[128,256]{1,0:T(8,128)S(1)} %get-tuple-element.39.after.refs_0_, ...), custom_call_target="tpu_custom_call" | custom-call | flops 30000001024 | tf_op jit(solution)/shard_map/attention/pallas_call | solution.py:291
  33.6 0.9 %collective-permute-start.16 = (bf16[128,256]{1,0:T(8,128)(2,1)S(1)}, bf16[128,256]{1,0:T(8,128)(2,1)S(1)}, u32[]{:S(2)}, u32[]{:S(2)}) collective-permute-start(bf16[128,256]{1,0:T(8,128)(2,1)S(1)} %get-tuple-element.42.refs_1_.refs_2_.grad), channel_id=1, source_target_pairs={{0,16},{8,24},{16,0},{24,8},{1,17},{9,25},{17,1},{25,9},{2,18},{10... | collective-permute-start | bytes 196616 | tf_op jit(solution)/shard_map/ppermute | solution.py:315
  35.2 1.1 %collective-permute-start.14 = (bf16[128,512]{1,0:T(8,128)(2,1)S(1)}, bf16[128,512]{1,0:T(8,128)(2,1)S(1)}, u32[]{:S(2)}, u32[]{:S(2)}) collective-permute-start(bf16[128,512]{1,0:T(8,128)(2,1)S(1)} %gate.11), channel_id=1, source_target_pairs={{0,24},{8,16},{16,8},{24,0},{1,25},{9,17},{17,9},{25,1},{2,26},{10... | collective-permute-start | bytes 393224 | tf_op jit(solution)/shard_map/ppermute | solution.py:315
  36.4 1.2 %collective-permute-start.24 = (bf16[1536,256]{1,0:T(8,128)(2,1)S(1)}, bf16[1536,256]{1,0:T(8,128)(2,1)S(1)}, u32[]{:S(2)}, u32[]{:S(2)}) collective-permute-start(bf16[1536,256]{1,0:T(8,128)(2,1)S(1)} %gather.1.refs_2_), channel_id=1, source_target_pairs={{0,16},{8,24},{16,0},{24,8},{1,17},{9,25},{17,1},{25,9},{2,18},{10... | collective-permute-start | bytes 2359304 | tf_op jit(solution)/shard_map/ppermute | solution.py:315
  39.3 1.5 %collective-permute-start.18 = (bf16[256,256]{1,0:T(8,128)(2,1)S(1)}, bf16[256,256]{1,0:T(8,128)(2,1)S(1)}, u32[]{:S(2)}, u32[]{:S(2)}) collective-permute-start(bf16[256,256]{1,0:T(8,128)(2,1)S(1)} %get-tuple-element.44.refs_6_), channel_id=1, source_target_pairs={{0,1},{1,0},{2,3},{3,2},{4,5},{5,4},{6,7},{7,6},{8,9},{9,8},{10,11... | collective-permute-start | bytes 393224 | tf_op jit(solution)/shard_map/ppermute | solution.py:315
  41.8 0.9 %collective-permute-start.19 = (bf16[512,256]{1,0:T(8,128)(2,1)S(1)}, bf16[512,256]{1,0:T(8,128)(2,1)S(1)}, u32[]{:S(2)}, u32[]{:S(2)}) collective-permute-start(bf16[512,256]{1,0:T(8,128)(2,1)S(1)} %gate.13), channel_id=1, source_target_pairs={{0,2},{1,3},{2,0},{3,1},{4,6},{5,7},{6,4},{7,5},{8,10},{9,11},{10,... | collective-permute-start | bytes 786440 | tf_op jit(solution)/shard_map/ppermute | solution.py:315
  42.6 1.5 %collective-permute-start.21 = (bf16[256,256]{1,0:T(8,128)(2,1)S(1)}, bf16[256,256]{1,0:T(8,128)(2,1)S(1)}, u32[]{:S(2)}, u32[]{:S(2)}) collective-permute-start(bf16[256,256]{1,0:T(8,128)(2,1)S(1)} %gate.15), channel_id=1, source_target_pairs={{0,1},{1,0},{2,3},{3,2},{4,5},{5,4},{6,7},{7,6},{8,9},{9,8},{10,11... | collective-permute-start | bytes 393224 | tf_op jit(solution)/shard_map/ppermute | solution.py:315
  44.2 1.4 %collective-permute-done.18.came = bf16[256,256]{1,0:T(8,128)(2,1)S(1)} collective-permute-done((bf16[256,256]{1,0:T(8,128)(2,1)S(1)}, bf16[256,256]{1,0:T(8,128)(2,1)S(1)}, u32[]{:S(2)}, u32[]{:S(2)}) %collective-permute-start.18) | collective-permute-done | bytes 131104 | tf_op jit(solution)/shard_map/ppermute | solution.py:315
  45.7 1.5 %collective-permute-start.20 = (bf16[256,256]{1,0:T(8,128)(2,1)S(1)}, bf16[256,256]{1,0:T(8,128)(2,1)S(1)}, u32[]{:S(2)}, u32[]{:S(2)}) collective-permute-start(bf16[256,256]{1,0:T(8,128)(2,1)S(1)} %pair.2.refs_6_.refs_1_), channel_id=1, source_target_pairs={{0,4},{1,5},{2,6},{3,7},{4,0},{5,1},{6,2},{7,3},{8,12},{9,13},{10,... | collective-permute-start | bytes 393224 | tf_op jit(solution)/shard_map/ppermute | solution.py:315
  47.5 0.9 %collective-permute-done.21.came = bf16[256,256]{1,0:T(8,128)(2,1)S(1)} collective-permute-done((bf16[256,256]{1,0:T(8,128)(2,1)S(1)}, bf16[256,256]{1,0:T(8,128)(2,1)S(1)}, u32[]{:S(2)}, u32[]{:S(2)}) %collective-permute-start.21) | collective-permute-done | bytes 131104 | tf_op jit(solution)/shard_map/ppermute | solution.py:315
  48.4 2.7 %collective-permute-start.22 = (bf16[256,256]{1,0:T(8,128)(2,1)S(1)}, bf16[256,256]{1,0:T(8,128)(2,1)S(1)}, u32[]{:S(2)}, u32[]{:S(2)}) collective-permute-start(bf16[256,256]{1,0:T(8,128)(2,1)S(1)} %pair.3.refs_1_), channel_id=1, source_target_pairs={{0,6},{1,7},{2,4},{3,5},{4,2},{5,3},{6,0},{7,1},{8,14},{9,15},{10,... | collective-permute-start | bytes 393224 | tf_op jit(solution)/shard_map/ppermute | solution.py:315
  51.1 1.4 %collective-permute-done.19.came = bf16[512,256]{1,0:T(8,128)(2,1)S(1)} collective-permute-done((bf16[512,256]{1,0:T(8,128)(2,1)S(1)}, bf16[512,256]{1,0:T(8,128)(2,1)S(1)}, u32[]{:S(2)}, u32[]{:S(2)}) %collective-permute-start.19) | collective-permute-done | bytes 262176 | tf_op jit(solution)/shard_map/ppermute | solution.py:315
  52.7 1.6 %collective-permute-start.23 = (bf16[256,256]{1,0:T(8,128)(2,1)S(1)}, bf16[256,256]{1,0:T(8,128)(2,1)S(1)}, u32[]{:S(2)}, u32[]{:S(2)}) collective-permute-start(bf16[256,256]{1,0:T(8,128)(2,1)S(1)} %gate.16), channel_id=1, source_target_pairs={{0,1},{1,0},{2,3},{3,2},{4,5},{5,4},{6,7},{7,6},{8,9},{9,8},{10,11... | collective-permute-start | bytes 393224 | tf_op jit(solution)/shard_map/ppermute | solution.py:315
  54.2 4.3 %collective-permute-done.20.refs_0_ = bf16[256,256]{1,0:T(8,128)(2,1)S(1)} collective-permute-done((bf16[256,256]{1,0:T(8,128)(2,1)S(1)}, bf16[256,256]{1,0:T(8,128)(2,1)S(1)}, u32[]{:S(2)}, u32[]{:S(2)}) %collective-permute-start.20) | collective-permute-done | bytes 131104 | tf_op jit(solution)/shard_map/ppermute | solution.py:315
  59.3 0.7 %input_grad.1 = (bf16[128,4096]{1,0:T(8,128)(2,1)S(1)}, bf16[128,4096]{1,0:T(8,128)(2,1)S(1)}) custom-call(bf16[256,256]{1,0:T(8,128)(2,1)S(1)} %total.1.after.refs_1_, bf16[128,256]{1,0:T(8,128)(2,1)S(1)} %get-tuple-element.42.refs_1_.refs_2_.grad, bf16[128,256]{1,0:T(8,128)(2,1)S(1)} %collective-permute-done.15.refs_3_.after.other, ...), custom_call_target="tpu_custom_call" | custom-call | tf_op jit(solution)/shard_map/input_grad/pallas_call | solution.py:291
  60.2 0.8 %rows.2.refs_1_.refs_0_ = f32[1024,256]{1,0:T(8,128)} custom-call(bf16[128,4096]{1,0:T(8,128)(2,1)S(1)} %get-tuple-element.52.mine.refs_0_, bf16[256,256]{1,0:T(8,128)(2,1)S(1)} %total.1.after.refs_1_, bf16[256,256]{1,0:T(8,128)(2,1)S(1)} %collective-permute-done.26.refs_2_), custom_call_target="tpu_custom_call" | custom-call | tf_op jit(solution)/shard_map/rows/pallas_call | solution.py:291
  61.1 3.5 %collective-permute-done.27.refs_0_ = bf16[256,256]{1,0:T(8,128)(2,1)S(1)} collective-permute-done((bf16[256,256]{1,0:T(8,128)(2,1)S(1)}, bf16[256,256]{1,0:T(8,128)(2,1)S(1)}, u32[]{:S(2)}, u32[]{:S(2)}) %collective-permute-start.27) | collective-permute-done | bytes 131104 | tf_op jit(solution)/shard_map/ppermute | solution.py:315
  64.6 1.5 %place.1.refs_1_ = bf16[128,8192]{1,0:T(8,128)(2,1)} custom-call(bf16[128,4096]{1,0:T(8,128)(2,1)S(1)} %get-tuple-element.52.mine.refs_0_, bf16[128,4096]{1,0:T(8,128)(2,1)S(1)} %collective-permute-done.25.came), custom_call_target="tpu_custom_call" | custom-call | flops 30000001024 | tf_op jit(solution)/shard_map/place/pallas_call | solution.py:291
  66.1 0.8 %rows.3 = f32[1024,256]{1,0:T(8,128)} custom-call(f32[1024,256]{1,0:T(8,128)} %rows.2.refs_1_.refs_0_, bf16[128,8192]{1,0:T(8,128)(2,1)} %place.1.refs_1_, bf16[256,256]{1,0:T(8,128)(2,1)S(1)} %gate.17.refs_2_, bf16[256,256]{1,0:T(8,128)(2,1)S(1)} %collective-permute-done.28.refs_3_), custom_call_target="tpu_custom_call", output_to_operand_aliasing={{}: (0, {})} | custom-call | tf_op jit(solution)/shard_map/rows/pallas_call | solution.py:291
  (56 shorter events, 9.8 us)
Async XLA Ops:
  0.6 10.3 %copy-start = (s32[1,128]{1,0:T(1,128)S(1)}, s32[1,128]{1,0:T(1,128)}, u32[]{:S(2)}) copy-start(s32[1,128]{1,0:T(1,128)} %seg_row.1) | copy-start | bytes 1540
  2.0 20.5 %collective-permute-start.6 = (bf16[256,1536]{1,0:T(8,128)(2,1)S(1)}, bf16[256,1536]{1,0:T(8,128)(2,1)S(1)}, u32[]{:S(2)}, u32[]{:S(2)}) collective-permute-start(bf16[256,1536]{1,0:T(8,128)(2,1)S(1)} %get-tuple-element.38), channel_id=1, source_target_pairs={{0,16},{8,24},{16,0},{24,8},{1,17},{9,25},{17,1},{25,9},{2,18},{10... | collective-permute-start | bytes 2359304 | tf_op jit(solution)/shard_map/ppermute | solution.py:315
  5.0 6.4 %collective-permute-start.1 = (bf16[256,256]{1,0:T(8,128)(2,1)S(1)}, bf16[256,256]{1,0:T(8,128)(2,1)S(1)}, u32[]{:S(2)}, u32[]{:S(2)}) collective-permute-start(bf16[256,256]{1,0:T(8,128)(2,1)S(1)} %get-tuple-element.31), channel_id=1, source_target_pairs={{0,2},{1,3},{2,0},{3,1},{4,6},{5,7},{6,4},{7,5},{8,10},{9,11},{10,... | collective-permute-start | bytes 393224 | tf_op jit(solution)/shard_map/ppermute | solution.py:315
  6.6 12.6 %collective-permute-start = (bf16[256,256]{1,0:T(8,128)(2,1)S(1)}, bf16[256,256]{1,0:T(8,128)(2,1)S(1)}, u32[]{:S(2)}, u32[]{:S(2)}) collective-permute-start(bf16[256,256]{1,0:T(8,128)(2,1)S(1)} %get-tuple-element.31), channel_id=1, source_target_pairs={{0,4},{1,5},{2,6},{3,7},{4,0},{5,1},{6,2},{7,3},{8,12},{9,13},{10,... | collective-permute-start | bytes 393224 | tf_op jit(solution)/shard_map/ppermute | solution.py:315
  9.2 11.6 %collective-permute-start.8 = (bf16[256,256]{1,0:T(8,128)(2,1)S(1)}, bf16[256,256]{1,0:T(8,128)(2,1)S(1)}, u32[]{:S(2)}, u32[]{:S(2)}) collective-permute-start(bf16[256,256]{1,0:T(8,128)(2,1)S(1)} %get-tuple-element.31), channel_id=1, source_target_pairs={{0,6},{1,7},{2,4},{3,5},{4,2},{5,3},{6,0},{7,1},{8,14},{9,15},{10,... | collective-permute-start | bytes 393224 | tf_op jit(solution)/shard_map/ppermute | solution.py:315
  9.4 12.1 %collective-permute-start.3 = (bf16[512,256]{1,0:T(8,128)(2,1)S(1)}, bf16[512,256]{1,0:T(8,128)(2,1)S(1)}, u32[]{:S(2)}, u32[]{:S(2)}) collective-permute-start(bf16[512,256]{1,0:T(8,128)(2,1)S(1)} %get-tuple-element.32.refs_1_.refs_0_), channel_id=1, source_target_pairs={{0,1},{1,0},{2,3},{3,2},{4,5},{5,4},{6,7},{7,6},{8,9},{9,8},{10,11... | collective-permute-start | bytes 786440 | tf_op jit(solution)/shard_map/ppermute | solution.py:315
  11.5 10.0 %collective-permute-start.2 = (bf16[256,256]{1,0:T(8,128)(2,1)S(1)}, bf16[256,256]{1,0:T(8,128)(2,1)S(1)}, u32[]{:S(2)}, u32[]{:S(2)}) collective-permute-start(bf16[256,256]{1,0:T(8,128)(2,1)S(1)} %collective-permute-done.1.refs_3_.refs_0_), channel_id=1, source_target_pairs={{0,1},{1,0},{2,3},{3,2},{4,5},{5,4},{6,7},{7,6},{8,9},{9,8},{10,11... | collective-permute-start | bytes 393224 | tf_op jit(solution)/shard_map/ppermute | solution.py:315
  19.3 5.0 %collective-permute-start.7 = (bf16[256,256]{1,0:T(8,128)(2,1)S(1)}, bf16[256,256]{1,0:T(8,128)(2,1)S(1)}, u32[]{:S(2)}, u32[]{:S(2)}) collective-permute-start(bf16[256,256]{1,0:T(8,128)(2,1)S(1)} %collective-permute-done.refs_1_.refs_5_.refs_2_), channel_id=1, source_target_pairs={{0,1},{1,0},{2,3},{3,2},{4,5},{5,4},{6,7},{7,6},{8,9},{9,8},{10,11... | collective-permute-start | bytes 393224 | tf_op jit(solution)/shard_map/ppermute | solution.py:315
  20.8 5.0 %collective-permute-start.9 = (bf16[256,256]{1,0:T(8,128)(2,1)S(1)}, bf16[256,256]{1,0:T(8,128)(2,1)S(1)}, u32[]{:S(2)}, u32[]{:S(2)}) collective-permute-start(bf16[256,256]{1,0:T(8,128)(2,1)S(1)} %collective-permute-done.8.refs_7_.refs_4_), channel_id=1, source_target_pairs={{0,1},{1,0},{2,3},{3,2},{4,5},{5,4},{6,7},{7,6},{8,9},{9,8},{10,11... | collective-permute-start | bytes 393224 | tf_op jit(solution)/shard_map/ppermute | solution.py:315
  21.5 4.3 %collective-permute-start.4 = (bf16[128,2560]{1,0:T(8,128)(2,1)S(1)}, bf16[128,2560]{1,0:T(8,128)(2,1)S(1)}, u32[]{:S(2)}, u32[]{:S(2)}) collective-permute-start(bf16[128,2560]{1,0:T(8,128)(2,1)S(1)} %gate.9), channel_id=1, source_target_pairs={{0,8},{8,0},{16,24},{24,16},{1,9},{9,1},{17,25},{25,17},{2,10},{10... | collective-permute-start | bytes 1966088 | tf_op jit(solution)/shard_map/ppermute | solution.py:315
  21.5 7.2 %collective-permute-start.5 = (bf16[128,512]{1,0:T(8,128)(2,1)S(1)}, bf16[128,512]{1,0:T(8,128)(2,1)S(1)}, u32[]{:S(2)}, u32[]{:S(2)}) collective-permute-start(bf16[128,512]{1,0:T(8,128)(2,1)S(1)} %gate.10), channel_id=1, source_target_pairs={{0,16},{8,24},{16,0},{24,8},{1,17},{9,25},{17,1},{25,9},{2,18},{10... | collective-permute-start | bytes 393224 | tf_op jit(solution)/shard_map/ppermute | solution.py:315
  22.6 4.4 %collective-permute-start.12 = (bf16[128,1536]{1,0:T(8,128)(2,1)S(1)}, bf16[128,1536]{1,0:T(8,128)(2,1)S(1)}, u32[]{:S(2)}, u32[]{:S(2)}) collective-permute-start(bf16[128,1536]{1,0:T(8,128)(2,1)S(1)} %hand_on.1), channel_id=1, source_target_pairs={{0,8},{8,0},{16,24},{24,16},{1,9},{9,1},{17,25},{25,17},{2,10},{10... | collective-permute-start | bytes 1179656 | tf_op jit(solution)/shard_map/ppermute | solution.py:315
  26.4 2.3 %collective-permute-start.10 = (bf16[128,256]{1,0:T(8,128)(2,1)S(1)}, bf16[128,256]{1,0:T(8,128)(2,1)S(1)}, u32[]{:S(2)}, u32[]{:S(2)}) collective-permute-start(bf16[128,256]{1,0:T(8,128)(2,1)S(1)} %get-tuple-element.40), channel_id=1, source_target_pairs={{0,8},{8,0},{16,24},{24,16},{1,9},{9,1},{17,25},{25,17},{2,10},{10... | collective-permute-start | bytes 196616 | tf_op jit(solution)/shard_map/ppermute | solution.py:315
  26.4 5.0 %collective-permute-start.11 = (bf16[128,256]{1,0:T(8,128)(2,1)S(1)}, bf16[128,256]{1,0:T(8,128)(2,1)S(1)}, u32[]{:S(2)}, u32[]{:S(2)}) collective-permute-start(bf16[128,256]{1,0:T(8,128)(2,1)S(1)} %get-tuple-element.41), channel_id=1, source_target_pairs={{0,16},{8,24},{16,0},{24,8},{1,17},{9,25},{17,1},{25,9},{2,18},{10... | collective-permute-start | bytes 196616 | tf_op jit(solution)/shard_map/ppermute | solution.py:315
  27.3 4.6 %collective-permute-start.13 = (bf16[128,256]{1,0:T(8,128)(2,1)S(1)}, bf16[128,256]{1,0:T(8,128)(2,1)S(1)}, u32[]{:S(2)}, u32[]{:S(2)}) collective-permute-start(bf16[128,256]{1,0:T(8,128)(2,1)S(1)} %project_last.1), channel_id=1, source_target_pairs={{0,24},{8,16},{16,8},{24,0},{1,25},{9,17},{17,9},{25,1},{2,26},{10... | collective-permute-start | bytes 196616 | tf_op jit(solution)/shard_map/ppermute | solution.py:315
  33.4 2.9 %collective-permute-start.15 = (bf16[128,256]{1,0:T(8,128)(2,1)S(1)}, bf16[128,256]{1,0:T(8,128)(2,1)S(1)}, u32[]{:S(2)}, u32[]{:S(2)}) collective-permute-start(bf16[128,256]{1,0:T(8,128)(2,1)S(1)} %get-tuple-element.42.refs_1_.refs_2_.grad), channel_id=1, source_target_pairs={{0,8},{8,0},{16,24},{24,16},{1,9},{9,1},{17,25},{25,17},{2,10},{10... | collective-permute-start | bytes 196616 | tf_op jit(solution)/shard_map/ppermute | solution.py:315
  33.6 4.6 %collective-permute-start.16 = (bf16[128,256]{1,0:T(8,128)(2,1)S(1)}, bf16[128,256]{1,0:T(8,128)(2,1)S(1)}, u32[]{:S(2)}, u32[]{:S(2)}) collective-permute-start(bf16[128,256]{1,0:T(8,128)(2,1)S(1)} %get-tuple-element.42.refs_1_.refs_2_.grad), channel_id=1, source_target_pairs={{0,16},{8,24},{16,0},{24,8},{1,17},{9,25},{17,1},{25,9},{2,18},{10... | collective-permute-start | bytes 196616 | tf_op jit(solution)/shard_map/ppermute | solution.py:315
  34.6 4.4 %collective-permute-start.17 = (bf16[128,256]{1,0:T(8,128)(2,1)S(1)}, bf16[128,256]{1,0:T(8,128)(2,1)S(1)}, u32[]{:S(2)}, u32[]{:S(2)}) collective-permute-start(bf16[128,256]{1,0:T(8,128)(2,1)S(1)} %get-tuple-element.42.refs_1_.refs_2_.grad), channel_id=1, source_target_pairs={{0,24},{8,16},{16,8},{24,0},{1,25},{9,17},{17,9},{25,1},{2,26},{10... | collective-permute-start | bytes 196616 | tf_op jit(solution)/shard_map/ppermute | solution.py:315
  35.2 6.5 %collective-permute-start.14 = (bf16[128,512]{1,0:T(8,128)(2,1)S(1)}, bf16[128,512]{1,0:T(8,128)(2,1)S(1)}, u32[]{:S(2)}, u32[]{:S(2)}) collective-permute-start(bf16[128,512]{1,0:T(8,128)(2,1)S(1)} %gate.11), channel_id=1, source_target_pairs={{0,24},{8,16},{16,8},{24,0},{1,25},{9,17},{17,9},{25,1},{2,26},{10... | collective-permute-start | bytes 393224 | tf_op jit(solution)/shard_map/ppermute | solution.py:315
  36.4 22.9 %collective-permute-start.24 = (bf16[1536,256]{1,0:T(8,128)(2,1)S(1)}, bf16[1536,256]{1,0:T(8,128)(2,1)S(1)}, u32[]{:S(2)}, u32[]{:S(2)}) collective-permute-start(bf16[1536,256]{1,0:T(8,128)(2,1)S(1)} %gather.1.refs_2_), channel_id=1, source_target_pairs={{0,16},{8,24},{16,0},{24,8},{1,17},{9,25},{17,1},{25,9},{2,18},{10... | collective-permute-start | bytes 2359304 | tf_op jit(solution)/shard_map/ppermute | solution.py:315
  39.3 6.3 %collective-permute-start.18 = (bf16[256,256]{1,0:T(8,128)(2,1)S(1)}, bf16[256,256]{1,0:T(8,128)(2,1)S(1)}, u32[]{:S(2)}, u32[]{:S(2)}) collective-permute-start(bf16[256,256]{1,0:T(8,128)(2,1)S(1)} %get-tuple-element.44.refs_6_), channel_id=1, source_target_pairs={{0,1},{1,0},{2,3},{3,2},{4,5},{5,4},{6,7},{7,6},{8,9},{9,8},{10,11... | collective-permute-start | bytes 393224 | tf_op jit(solution)/shard_map/ppermute | solution.py:315
  41.8 10.8 %collective-permute-start.19 = (bf16[512,256]{1,0:T(8,128)(2,1)S(1)}, bf16[512,256]{1,0:T(8,128)(2,1)S(1)}, u32[]{:S(2)}, u32[]{:S(2)}) collective-permute-start(bf16[512,256]{1,0:T(8,128)(2,1)S(1)} %gate.13), channel_id=1, source_target_pairs={{0,2},{1,3},{2,0},{3,1},{4,6},{5,7},{6,4},{7,5},{8,10},{9,11},{10,... | collective-permute-start | bytes 786440 | tf_op jit(solution)/shard_map/ppermute | solution.py:315
  42.6 5.8 %collective-permute-start.21 = (bf16[256,256]{1,0:T(8,128)(2,1)S(1)}, bf16[256,256]{1,0:T(8,128)(2,1)S(1)}, u32[]{:S(2)}, u32[]{:S(2)}) collective-permute-start(bf16[256,256]{1,0:T(8,128)(2,1)S(1)} %gate.15), channel_id=1, source_target_pairs={{0,1},{1,0},{2,3},{3,2},{4,5},{5,4},{6,7},{7,6},{8,9},{9,8},{10,11... | collective-permute-start | bytes 393224 | tf_op jit(solution)/shard_map/ppermute | solution.py:315
  45.7 12.9 %collective-permute-start.20 = (bf16[256,256]{1,0:T(8,128)(2,1)S(1)}, bf16[256,256]{1,0:T(8,128)(2,1)S(1)}, u32[]{:S(2)}, u32[]{:S(2)}) collective-permute-start(bf16[256,256]{1,0:T(8,128)(2,1)S(1)} %pair.2.refs_6_.refs_1_), channel_id=1, source_target_pairs={{0,4},{1,5},{2,6},{3,7},{4,0},{5,1},{6,2},{7,3},{8,12},{9,13},{10,... | collective-permute-start | bytes 393224 | tf_op jit(solution)/shard_map/ppermute | solution.py:315
  48.4 10.1 %collective-permute-start.22 = (bf16[256,256]{1,0:T(8,128)(2,1)S(1)}, bf16[256,256]{1,0:T(8,128)(2,1)S(1)}, u32[]{:S(2)}, u32[]{:S(2)}) collective-permute-start(bf16[256,256]{1,0:T(8,128)(2,1)S(1)} %pair.3.refs_1_), channel_id=1, source_target_pairs={{0,6},{1,7},{2,4},{3,5},{4,2},{5,3},{6,0},{7,1},{8,14},{9,15},{10,... | collective-permute-start | bytes 393224 | tf_op jit(solution)/shard_map/ppermute | solution.py:315
  52.7 5.9 %collective-permute-start.23 = (bf16[256,256]{1,0:T(8,128)(2,1)S(1)}, bf16[256,256]{1,0:T(8,128)(2,1)S(1)}, u32[]{:S(2)}, u32[]{:S(2)}) collective-permute-start(bf16[256,256]{1,0:T(8,128)(2,1)S(1)} %gate.16), channel_id=1, source_target_pairs={{0,1},{1,0},{2,3},{3,2},{4,5},{5,4},{6,7},{7,6},{8,9},{9,8},{10,11... | collective-permute-start | bytes 393224 | tf_op jit(solution)/shard_map/ppermute | solution.py:315
  58.6 1.6 %collective-permute-start.26 = (bf16[256,256]{1,0:T(8,128)(2,1)S(1)}, bf16[256,256]{1,0:T(8,128)(2,1)S(1)}, u32[]{:S(2)}, u32[]{:S(2)}) collective-permute-start(bf16[256,256]{1,0:T(8,128)(2,1)S(1)} %total.1.after.refs_1_), channel_id=1, source_target_pairs={{0,8},{8,0},{16,24},{24,16},{1,9},{9,1},{17,25},{25,17},{2,10},{10... | collective-permute-start | bytes 393224 | tf_op jit(solution)/shard_map/ppermute | solution.py:315
  58.7 5.9 %collective-permute-start.27 = (bf16[256,256]{1,0:T(8,128)(2,1)S(1)}, bf16[256,256]{1,0:T(8,128)(2,1)S(1)}, u32[]{:S(2)}, u32[]{:S(2)}) collective-permute-start(bf16[256,256]{1,0:T(8,128)(2,1)S(1)} %total.1.after.refs_1_), channel_id=1, source_target_pairs={{0,16},{8,24},{16,0},{24,8},{1,17},{9,25},{17,1},{25,9},{2,18},{10... | collective-permute-start | bytes 393224 | tf_op jit(solution)/shard_map/ppermute | solution.py:315
  60.0 4.6 %collective-permute-start.25 = (bf16[128,4096]{1,0:T(8,128)(2,1)S(1)}, bf16[128,4096]{1,0:T(8,128)(2,1)S(1)}, u32[]{:S(2)}, u32[]{:S(2)}) collective-permute-start(bf16[128,4096]{1,0:T(8,128)(2,1)S(1)} %get-tuple-element.53), channel_id=1, source_target_pairs={{0,8},{8,0},{16,24},{24,16},{1,9},{9,1},{17,25},{25,17},{2,10},{10... | collective-permute-start | bytes 3145736 | tf_op jit(solution)/shard_map/ppermute | solution.py:315
  64.6 1.5 %collective-permute-start.28 = (bf16[256,256]{1,0:T(8,128)(2,1)S(1)}, bf16[256,256]{1,0:T(8,128)(2,1)S(1)}, u32[]{:S(2)}, u32[]{:S(2)}) collective-permute-start(bf16[256,256]{1,0:T(8,128)(2,1)S(1)} %gate.17.refs_2_), channel_id=1, source_target_pairs={{0,8},{8,0},{16,24},{24,16},{1,9},{9,1},{17,25},{25,17},{2,10},{10... | collective-permute-start | bytes 393224 | tf_op jit(solution)/shard_map/ppermute | solution.py:315
